TPU v7x, 32 devices: a whole 2x2x4 slice. The times are simulated.
32 devices in a mesh: bin: 8 (over y, x, core), coil: 4 (over z).
Axes of the slice: x: 2, y: 2, z: 4, core: 2. Of those that a mesh axis runs over, the one named last changes fastest.
Arguments:
- cine_image: bfloat16 [8, 256, 8, 256], P('bin', 'coil'), may hold values from -6 to 6
- warp_blocks: bfloat16 [8, 4096, 2, 4096], P('bin', 'coil'), may hold values from -0.5 to 0.5
- warp_index: int32 [8, 4096, 2], P('bin', 'coil'), may hold values from 0 to 4095, as said below
- sample_mask: int32 [8, 256, 128], P('bin'), may hold values 0 or 1
- kspace_data: bfloat16 [8, 8, 256, 8, 256], P('bin', 'coil'), may hold values from -6 to 6
- sensitivity: bfloat16 [8, 256, 8, 256], P(None, 'coil'), may hold values from -1.5 to 1.5
Outputs:
- gradient: float32 [8, 256, 8, 256], P('bin', 'coil')
Inputs may be any that keep to these rules, and one draw needn't show every extreme that they name: `warp_index`: slot 0 of every block names the block itself; every other slot of the block at row y names a block whose row lies among the 16 rows from 16 * (y // 16) on.
All inputs are finite; a program needn't handle non-finite values. No bound on the sum of `sample_mask` on one device may be relied on, other than what follows from the above.
Results may differ from a plain program's by a relative error of at most 0.017.
Values may be sent and summed in bfloat16 or wider, within the bound.
A program may use at most 128 MiB of HBM per device.

v0:
```python
import jax
import jax.numpy as jnp
from jax import lax
from jax.sharding import PartitionSpec as P

NY = 256
NX = 128
BLOCK = 64


def shifted(block, axis, distance):
    devices = range(lax.axis_size(axis))
    route = [((i - distance) % len(devices), i) for i in devices]
    return lax.ppermute(block, axis, route)


def cosine_sine(length):
    positions = jnp.arange(length, dtype=jnp.int32)
    phases = positions[:, None] * positions[None, :] % length
    angles = phases.astype(jnp.float32) * (2.0 * jnp.pi / length)
    factor = 1.0 / jnp.sqrt(jnp.asarray(length, jnp.float32))
    return (jnp.cos(angles) * factor, jnp.sin(angles) * factor)


def make_row_matrix(length):
    cosine_table, sine_table = cosine_sine(length)
    upper_half = jnp.concatenate([cosine_table, -sine_table], axis=1)
    lower_half = jnp.concatenate([sine_table, cosine_table], axis=1)
    return jnp.concatenate([upper_half, lower_half], axis=0).astype(jnp.bfloat16)


def make_column_tables(length):
    cosine_table, sine_table = cosine_sine(length)
    return jnp.stack([cosine_table, sine_table]).astype(jnp.bfloat16)


def row_apply(values, row_matrix, inverse):
    flattened = values.reshape(-1, values.shape[-1])
    table_used = row_matrix.T if inverse else row_matrix
    return jnp.dot(flattened, table_used, preferred_element_type=jnp.float32).reshape(values.shape)


def column_transform(values, tables, inverse):
    products = jnp.einsum("tky,cyzx->tckzx", tables, values, preferred_element_type=jnp.float32)
    direct, turned = (products[0], products[1])
    half_width = direct.shape[-1] // 2
    if inverse:
        swapped = jnp.concatenate([-turned[..., half_width:], turned[..., :half_width]], axis=-1)
    else:
        swapped = jnp.concatenate([turned[..., half_width:], -turned[..., :half_width]], axis=-1)
    return direct + swapped


def coil_images(sensitivity, moved_image):
    half_width = moved_image.shape[-1] // 2
    sens_re = sensitivity[..., :half_width].astype(jnp.float32)
    sens_im = sensitivity[..., half_width:].astype(jnp.float32)
    image_re = moved_image[..., :half_width].astype(jnp.float32)
    image_im = moved_image[..., half_width:].astype(jnp.float32)
    real_part = sens_re * image_re - sens_im * image_im
    imag_part = sens_re * image_im + sens_im * image_re
    return jnp.concatenate([real_part, imag_part], axis=-1).astype(jnp.bfloat16)


def conj_sum(sensitivity, back_rows):
    half_width = back_rows.shape[-1] // 2
    sens_re = sensitivity[..., :half_width].astype(jnp.float32)
    sens_im = sensitivity[..., half_width:].astype(jnp.float32)
    back_re = back_rows[..., :half_width]
    back_im = back_rows[..., half_width:]
    real_part = jnp.sum(sens_re * back_re + sens_im * back_im, axis=0)
    imag_part = jnp.sum(sens_re * back_im - sens_im * back_re, axis=0)
    return jnp.concatenate([real_part, imag_part], axis=-1)


def column_part(row_spectra, measured, mask_now, column_tables):
    spectra = column_transform(row_spectra, column_tables, False)
    weight_mask = jnp.concatenate([mask_now, mask_now], axis=1).astype(jnp.float32)[:, None, :]
    residual = (weight_mask * (spectra - measured.astype(jnp.float32))).astype(jnp.bfloat16)
    return column_transform(residual, column_tables, True).astype(jnp.bfloat16)


def split_blocks(values):
    row_count, depth_count, full_width = values.shape
    grouped = values.reshape(row_count, depth_count, 2, full_width // (2 * BLOCK), BLOCK)
    return grouped.transpose(0, 1, 3, 2, 4).reshape(-1, 2, BLOCK)


def join_blocks(pieces, row_count, depth_count, full_width):
    grouped = pieces.reshape(row_count, depth_count, full_width // (2 * BLOCK), 2, BLOCK)
    return grouped.transpose(0, 1, 3, 2, 4).reshape(row_count, depth_count, full_width)


def warp_forward(source, weights, block_index):
    pieces = split_blocks(source)
    chosen = jnp.take(pieces, block_index, axis=0)
    matrices = weights.reshape(weights.shape[0], weights.shape[1], BLOCK, BLOCK)
    return jnp.einsum("ikpq,ikcq->icp", matrices, chosen, preferred_element_type=jnp.float32)


def warp_adjoint(values, weights, block_index):
    block_count, slots = block_index.shape
    matrices = weights.reshape(block_count, slots, BLOCK, BLOCK)
    contributions = jnp.einsum(
        "ikpq,icp->ikcq", matrices, values, preferred_element_type=jnp.float32
    )
    targets = jnp.arange(block_count, dtype=jnp.int32)
    selector = (block_index.reshape(1, -1) == targets[:, None]).astype(jnp.float32)
    summed = jnp.dot(
        selector,
        contributions.reshape(block_count * slots, 2 * BLOCK),
        precision=lax.Precision.HIGHEST,
    )
    return summed.reshape(block_count, 2, BLOCK)


def on_device(cine_image, warp_blocks, warp_index, sample_mask, kspace_data, sensitivity):
    current = cine_image[0]
    row_count, depth_count, full_width = current.shape
    row_matrix = make_row_matrix(NX)
    column_tables = make_column_tables(NY)
    earlier = shifted(cine_image, "bin", 1)[0]
    block_count = warp_index.shape[1]
    local_index = warp_index[0] - lax.axis_index("coil") * block_count
    weights = warp_blocks[0]
    warped = join_blocks(
        warp_forward(earlier, weights, local_index), row_count, depth_count, full_width
    )
    moved_image = (current.astype(jnp.float32) + warped).astype(jnp.bfloat16)
    measured = kspace_data[0]
    mask_now = sample_mask[0]
    coil_sens = lax.all_to_all(sensitivity, "coil", split_axis=0, concat_axis=1, tiled=True)
    sens_rows = coil_sens
    images = coil_images(sens_rows, lax.all_gather(moved_image, "coil", axis=0, tiled=True))
    own_coils = row_apply(images, row_matrix, False).astype(jnp.bfloat16)
    back_columns = column_part(own_coils, measured, mask_now, column_tables)
    sens_rows = coil_sens
    data_grad = lax.psum_scatter(
        conj_sum(sens_rows, row_apply(back_columns, row_matrix, True)).astype(jnp.bfloat16),
        "coil",
        scatter_dimension=0,
        tiled=True,
    ).astype(jnp.float32)
    pieces = split_blocks(data_grad.astype(jnp.bfloat16))
    pulled = join_blocks(
        warp_adjoint(pieces, weights, local_index), row_count, depth_count, full_width
    ).astype(jnp.bfloat16)
    from_next = shifted(pulled, "bin", -1)
    return (data_grad + from_next.astype(jnp.float32))[None]


def solution(mesh):
    return jax.shard_map(
        on_device,
        mesh=mesh,
        in_specs=(
            P("bin", "coil", None, None),
            P("bin", "coil", None, None),
            P("bin", "coil", None),
            P("bin", None, None),
            P("bin", "coil", None, None, None),
            P(None, "coil", None, None),
        ),
        out_specs=P("bin", "coil", None, None),
        check_vma=False,
    )
```

profile of v0, /device:TPU:0, one launch (start us, length us, event | category | flops | bytes accessed | tf_op | source)
XLA Modules:
  0.0 253.3 jit_solution(12267860992231000962)
XLA Ops:
  7.0 6.0 %all-to-all-start = ((bf16[8,64,8,256]{3,2,1,0:T(8,128)(2,1)}), bf16[8,64,8,256]{3,2,1,0:T(8,128)(2,1)S(1)}, u32[]{:S(2)}, u32[]{:S(2)}) async-start(bf16[8,64,8,256]{3,2,1,0:T(8,128)(2,1)} %param.11), calls=%async_computation | async-start | bytes 4194304 | tf_op jit(solution)/shard_map/all_to_all | solution.py:132
  13.5 40.9 %copy.66 = bf16[1,1024,2,4096]{1,3,2,0:T(8,128)(2,1)} copy(bf16[1,1024,2,4096]{3,2,1,0:T(2,128)(2,1)} %param.7) | data formatting | bytes 33554432 | tf_op args[1]
  54.4 46.0 %copy.67 = bf16[1024,2,64,64]{3,2,1,0:T(8,128)(2,1)} copy(bf16[1024,2,64,64]{0,3,2,1:T(8,128)(2,1)} %bitcast.123) | data formatting | bytes 33554432 | tf_op jit(solution)/shard_map/reshape;squeeze | solution.py:97
  101.9 13.8 %gather_fusion = bf16[2048,2,64]{2,1,0:T(2,128)(2,1)} fusion(bf16[1024,2,64]{2,1,0:T(2,128)(2,1)S(1)} %copy.65, s32[2048]{0:T(1024)S(1)} %broadcast_clamp_fusion), kind=kCustom, calls=%fused_computation | custom fusion | bytes 1056768 | tf_op jit(solution)/shard_map/jit(_take)/gather | solution.py:96
  115.7 15.8 %fusion.41 = f32[1024,2,64,1]{2,1,3,0:T(2,128)} fusion(bf16[1024,2,64,64]{3,2,1,0:T(8,128)(2,1)} %copy.67, bf16[1024,2,2,64]{3,2,1,0:T(2,128)(2,1)} %bitcast.133, pred[1024,2]{1,0:T(8,128)(4,1)S(1)} %copy.62), kind=kOutput, calls=%fused_computation.50 | convolution fusion | flops 33816576 | bytes 17827840 | tf_op jit(solution)/shard_map/ikpq,ikcq->icp/dot_general | solution.py:98
  131.5 1.8 copy.68
  133.3 1.6 reshape.199
  134.9 1.8 fusion.42
  137.0 4.3 %copy.73 = bf16[1,2,256,8,256]{2,4,3,1,0:T(8,128)(2,1)} copy(bf16[1,2,256,8,256]{4,3,2,1,0:T(8,128)(2,1)} %param.10) | data formatting | bytes 4194304 | tf_op args[4]
  141.5 0.9 fusion.56
  142.3 0.9 negate_convert_fusion
  143.3 1.7 multiply_convert_fusion
  145.0 21.3 %all-gather.2.cloned.1.call-done = bf16[256,8,256]{2,1,0:T(8,128)(2,1)} async-done(((bf16[64,8,256]{2,1,0:T(8,128)(2,1)}), bf16[256,8,256]{2,1,0:T(8,128)(2,1)}) %all-gather.2.cloned.1.call-update) | async-done | bytes 1048592 | tf_op jit(solution)/shard_map/all_gather | solution.py:134
  166.3 1.3 slice_convert_fusion.1
  167.9 1.2 copy.70
  169.1 1.3 copy-done.1
  170.4 2.2 copy.60
  172.6 2.0 fusion.12
  174.6 6.6 %convolution_bitcast_fusion.1 = f32[2,2,256,8,256]{2,4,0,3,1:T(8,128)} fusion(bf16[2,256,8,128]{3,1,2,0:T(8,128)(2,1)} %get-tuple-element.14, bf16[2,256,8,128]{3,1,2,0:T(8,128)(2,1)} %get-tuple-element.13, bf16[1,256,256]{2,1,0:T(8,128)(2,1)S(1)} %get-tuple-element.17, bf16[1,256,256]{2,1,0:T(8,128)(2,1)} %get-tuple-element.18, ...), kind=kOutput, calls=%fused_computation.25 | convolution fusion | flops 1616904192 | bytes 10846208 | tf_op jit(solution)/shard_map/tky,cyzx->tckzx/dot_general | solution.py:44
  181.2 2.7 %slice_bitcast_fusion.2 = f32[2,256,8,256]{1,3,2,0:T(8,128)S(1)} fusion(f32[2,2,256,8,256]{2,4,0,3,1:T(8,128)} %convolution_bitcast_fusion.1), kind=kLoop, calls=%fused_computation.8 | loop fusion | bytes 8388608 | tf_op jit(solution)/shard_map/squeeze | solution.py:45
  184.7 1.7 slice-done.1
  186.9 1.3 convolution_bitcast_fusion
  189.4 0.9 fusion.21
  191.1 1.1 pad_maximum_fusion
  192.8 26.3 %reduce-scatter.2.cloned.1.call-done = bf16[64,8,256]{2,0,1:T(8,128)(2,1)} async-done(((bf16[256,8,256]{2,0,1:T(8,128)(2,1)}), bf16[64,8,256]{2,0,1:T(8,128)(2,1)}) %reduce-scatter.2.cloned.1.call-update) | async-done | bytes 262160 | tf_op jit(solution)/shard_map/reduce_scatter | solution.py:138
  219.1 1.2 reshape.200
  220.8 13.1 %convolution_bitcast_fusion.2 = f32[1024,2,2,64]{3,2,1,0:T(2,128)S(1)} fusion(bf16[1024,2,64,1]{2,1,3,0:T(2,128)(2,1)S(1)} %bitcast.130, bf16[1024,2,64,64]{3,2,1,0:T(8,128)(2,1)} %copy.67), kind=kOutput, calls=%fused_computation.47 | convolution fusion | flops 33554432 | bytes 18087936 | tf_op jit(solution)/shard_map/ikpq,icp->ikcq/dot_general | solution.py:104
  233.9 1.1 reshape.202
  235.4 3.6 %fusion.38 = bf16[64,8,2,2,64]{4,1,2,3,0:T(8,128)(2,1)S(1)} fusion(f32[2,64,2048,1,1]{2,1,0,4,3:T(8,128)S(1)} %bitcast.134, s32[64,8,2]{1,2,0:T(2,128)S(1)} %multiply_add_fusion, s32[2048]{0:T(1024)S(1)} %sub.44), kind=kOutput, calls=%fused_computation.49 | convolution fusion | flops 3223453696 | bytes 1323008 | tf_op jit(solution)/shard_map/dot_general | solution.py:109
  239.7 1.7 collective-permute-start.1
  241.4 3.9 %collective-permute-done.1 = bf16[64,8,256]{2,0,1:T(8,128)(2,1)S(1)} collective-permute-done((bf16[64,8,256]{2,0,1:T(8,128)(2,1)S(1)}, bf16[64,8,256]{2,0,1:T(8,128)(2,1)S(1)}, u32[]{:S(2)}, u32[]{:S(2)}) %collective-permute-start.1) | collective-permute-done | bytes 262176 | tf_op jit(solution)/shard_map/ppermute | solution.py:14
  245.4 1.1 copy.82
  (56 shorter events, 8.3 us)
Async XLA Ops:
  6.5 6.5 %copy-start.10 = (s32[1,1024,2]{1,2,0:T(2,128)S(1)}, s32[1,1024,2]{1,2,0:T(2,128)}, u32[]{:S(2)}) copy-start(s32[1,1024,2]{1,2,0:T(2,128)} %param.8) | copy-start | bytes 24580
  6.5 94.2 %collective-permute-start = (bf16[1,64,8,256]{3,2,1,0:T(8,128)(2,1)}, bf16[1,64,8,256]{3,2,1,0:T(8,128)(2,1)S(1)}, u32[]{:S(2)}, u32[]{:S(2)}) collective-permute-start(bf16[1,64,8,256]{3,2,1,0:T(8,128)(2,1)} %param.6), channel_id=1, source_target_pairs={{28,0},{0,4},{4,8},{8,12},{12,16},{16,20},{20,24},{24,28},{29,1},{... | collective-permute-start | bytes 786440 | tf_op jit(solution)/shard_map/ppermute | solution.py:14
  7.0 162.1 %all-to-all-start = ((bf16[8,64,8,256]{3,2,1,0:T(8,128)(2,1)}), bf16[8,64,8,256]{3,2,1,0:T(8,128)(2,1)S(1)}, u32[]{:S(2)}, u32[]{:S(2)}) async-start(bf16[8,64,8,256]{3,2,1,0:T(8,128)(2,1)} %param.11), calls=%async_computation | async-start | bytes 4194304 | tf_op jit(solution)/shard_map/all_to_all | solution.py:132
  13.0 153.3 %all-gather.2.cloned.1.call-start = ((), (), s32[]{:S(2)}) async-start(), calls=%async_computation.2 | async-start | bytes 1310720 | tf_op jit(solution)/shard_map/all_gather | solution.py:134
  131.5 3.4 %copy-start.8 = (bf16[1,64,8,256]{3,2,1,0:T(8,128)(2,1)S(1)}, bf16[1,64,8,256]{3,2,1,0:T(8,128)(2,1)}, u32[]{:S(2)}) copy-start(bf16[1,64,8,256]{3,2,1,0:T(8,128)(2,1)} %param.6) | copy-start | bytes 786436
  136.8 4.6 %copy-start.9 = (s32[1,256,128]{2,1,0:T(8,128)S(1)}, s32[1,256,128]{2,1,0:T(8,128)}, u32[]{:S(2)}) copy-start(s32[1,256,128]{2,1,0:T(8,128)} %param.9) | copy-start | bytes 393220
  136.8 82.4 %reduce-scatter.2.cloned.1.call-start = ((), (), s32[]{:S(2)}) async-start(), calls=%async_computation.3 | async-start | bytes 1310720 | tf_op jit(solution)/shard_map/reduce_scatter | solution.py:138
  169.1 1.3 copy-start.1
  170.4 2.2 copy-start.2
  181.2 3.5 %slice-start = ((s8[8388608]{0:T(1024)(128)(4,1)}), s8[4194304]{0:T(1024)(128)(4,1)S(1)}, s32[]{:S(2)}) async-start(s8[8388608]{0:T(1024)(128)(4,1)} %bitcast.124), calls=%async_computation.4 | async-start | bytes 8388608
  184.0 2.4 slice-start.1
  184.0 2.9 %copy-start = (bf16[1,2,256,8,256]{2,4,3,1,0:T(8,128)(2,1)S(1)}, bf16[1,2,256,8,256]{2,4,3,1,0:T(8,128)(2,1)}, u32[]{:S(2)}) copy-start(bf16[1,2,256,8,256]{2,4,3,1,0:T(8,128)(2,1)} %copy.73) | copy-start | bytes 6291460
  184.0 2.9 %copy-start.3 = (bf16[1,256,256]{2,1,0:T(8,128)(2,1)S(1)}, bf16[1,256,256]{2,1,0:T(8,128)(2,1)}, u32[]{:S(2)}) copy-start(bf16[1,256,256]{2,1,0:T(8,128)(2,1)} %get-tuple-element.18) | copy-start | bytes 393220
  188.7 0.8 copy-start.5
  188.7 0.8 copy-start.6
  188.7 0.8 copy-start.7
  235.4 10.0 %copy-start.4 = (bf16[64,8,256]{2,0,1:T(8,128)(2,1)S(1)}, bf16[64,8,256]{2,0,1:T(8,128)(2,1)}, u32[]{:S(2)}) copy-start(bf16[64,8,256]{2,0,1:T(8,128)(2,1)} %reduce-scatter.2.cloned.1.call-done) | copy-start | bytes 786436
  239.7 5.6 %collective-permute-start.1 = (bf16[64,8,256]{2,0,1:T(8,128)(2,1)S(1)}, bf16[64,8,256]{2,0,1:T(8,128)(2,1)S(1)}, u32[]{:S(2)}, u32[]{:S(2)}) collective-permute-start(bf16[64,8,256]{2,0,1:T(8,128)(2,1)S(1)} %reshape.222), channel_id=1, source_target_pairs={{4,0},{8,4},{12,8},{16,12},{20,16},{24,20},{28,24},{0,28},{5,1},{9... | collective-permute-start | bytes 786440 | tf_op jit(solution)/shard_map/ppermute | solution.py:14
Sparse Core Ops, SparseCore 0:
  136.9 29.3 all-gather.1
  192.4 26.7 reduce-scatter.1
where the time goes:
time: 256 us; the launch traced here: 253 us
  local copies, waits for them, and re-layouts  127 us (50%)
  waiting for transfers between devices  51.6 us (20%)
  matrix products  41.3 us (16%)
  between operations  13.7 us (5%)
  other arithmetic  11.6 us (5%)
  starting transfers between devices  8.39 us (3%)
    unnamed x28, local copies, waits for them, and re-layouts  49.4 us
    another operation x1, local copies, waits for them, and re-layouts, warp_forward(): matrices = weights.reshape(weights.shape[0], weights.shape[1], BLOCK, BLOCK)  46 us
    reduce_scatter x1, waiting for transfers between devices, on_device(): lax.psum_scatter(conj_sum(sens_rows, row_apply(back_columns, row_matrix,...  26.3 us
    all_gather x1, waiting for transfers between devices, on_device(): lax.all_gather(moved_image, 'coil', axis=0, tiled=True)  21.3 us
    dot_general x1, matrix products, warp_forward(): jnp.einsum('ikpq,ikcq->icp', matrices, chosen, preferred_element_type=jnp...  15.8 us
    gather x1, local copies, waits for them, and re-layouts, warp_forward(): chosen = jnp.take(pieces, block_index, axis=0)  13.8 us
    dot_general x1, matrix products, warp_adjoint(): jnp.einsum('ikpq,icp->ikcq', matrices, values, preferred_element_type=jnp...  13.1 us
    dot_general x2, matrix products, column_transform(): jnp.einsum('tky,cyzx->tckzx', tables, values, preferred_element_type=jnp....  7.94 us
  transfers between devices with their start and end apart: 5, of which 3 were waited for; matrix products, arithmetic and copies ran while one was open for 53% of the time, Pallas kernels for 0%

commit v1 on v0

--- a/solution.py
+++ b/solution.py
@@ -1,11 +1,15 @@
 import jax
 import jax.numpy as jnp
 from jax import lax
+from jax.experimental import pallas as pl
+from jax.experimental.pallas import tpu as pltpu
 from jax.sharding import PartitionSpec as P
 
 NY = 256
 NX = 128
 BLOCK = 64
+LANES = 128
+ROWS = 128
 
 
 def shifted(block, axis, distance):
@@ -80,38 +84,213 @@
     return column_transform(residual, column_tables, True).astype(jnp.bfloat16)
 
 
-def split_blocks(values):
-    row_count, depth_count, full_width = values.shape
-    grouped = values.reshape(row_count, depth_count, 2, full_width // (2 * BLOCK), BLOCK)
-    return grouped.transpose(0, 1, 3, 2, 4).reshape(-1, 2, BLOCK)
-
-
-def join_blocks(pieces, row_count, depth_count, full_width):
-    grouped = pieces.reshape(row_count, depth_count, full_width // (2 * BLOCK), 2, BLOCK)
-    return grouped.transpose(0, 1, 3, 2, 4).reshape(row_count, depth_count, full_width)
-
-
-def warp_forward(source, weights, block_index):
-    pieces = split_blocks(source)
-    chosen = jnp.take(pieces, block_index, axis=0)
-    matrices = weights.reshape(weights.shape[0], weights.shape[1], BLOCK, BLOCK)
-    return jnp.einsum("ikpq,ikcq->icp", matrices, chosen, preferred_element_type=jnp.float32)
-
-
-def warp_adjoint(values, weights, block_index):
-    block_count, slots = block_index.shape
-    matrices = weights.reshape(block_count, slots, BLOCK, BLOCK)
-    contributions = jnp.einsum(
-        "ikpq,icp->ikcq", matrices, values, preferred_element_type=jnp.float32
-    )
-    targets = jnp.arange(block_count, dtype=jnp.int32)
-    selector = (block_index.reshape(1, -1) == targets[:, None]).astype(jnp.float32)
-    summed = jnp.dot(
-        selector,
-        contributions.reshape(block_count * slots, 2 * BLOCK),
-        precision=lax.Precision.HIGHEST,
-    )
-    return summed.reshape(block_count, 2, BLOCK)
+def one_hot(test):
+    return jnp.where(test, 1.0, 0.0).astype(jnp.bfloat16)
+
+
+def turn(values):
+    return pltpu.roll(values, BLOCK, 1)
+
+
+def strips_to_parts(first, second, low):
+    return jnp.where(low, first, turn(second)), jnp.where(low, turn(first), second)
+
+
+def forward_kernel(w_ref, earlier_ref, current_ref, index_ref, out_ref, source_ref):
+    f32, bf16 = jnp.float32, jnp.bfloat16
+    rows = ROWS
+    low = lax.broadcasted_iota(jnp.int32, (rows, LANES), 1) < BLOCK
+    earlier = earlier_ref[...].astype(f32)
+    own = (earlier[:, :LANES], earlier[:, LANES:])
+    pieces = jnp.concatenate(strips_to_parts(own[0], own[1], low), axis=0).astype(bf16)
+    numbers = lax.broadcasted_iota(jnp.int32, (rows, 2 * rows), 1)
+    index = index_ref[...]
+    chosen = [
+        jnp.dot(one_hot(index[:, s : s + 1] == numbers), pieces, preferred_element_type=f32)
+        for s in range(2)
+    ]
+    other = strips_to_parts(chosen[0], chosen[1], low)
+    for k, image in enumerate((own, other)):
+        for c in range(2):
+            plain, turned = image[c], turn(image[c])
+            zero = jnp.zeros_like(plain)
+            base = k * 4 + c * 2
+            source_ref[base, :, :LANES] = jnp.where(low, plain, 0.0)
+            source_ref[base + 1, :, :LANES] = jnp.where(low, 0.0, turned)
+            source_ref[base + 8, :, LANES:] = jnp.where(low, turned, 0.0)
+            source_ref[base + 9, :, LANES:] = jnp.where(low, 0.0, plain)
+            for h in range(2):
+                source_ref[base + h, :, LANES:] = zero
+                source_ref[base + 8 + h, :, :LANES] = zero
+
+    lane = lax.broadcasted_iota(jnp.int32, (BLOCK, LANES), 1)
+    row = lax.broadcasted_iota(jnp.int32, (BLOCK, LANES), 0)
+    same_slot = row % 2 == lane // 32 % 2
+    spot = lane % 8
+    er = lax.broadcasted_iota(jnp.int32, (BLOCK, 2 * LANES), 0)
+    el = lax.broadcasted_iota(jnp.int32, (BLOCK, 2 * LANES), 1)
+    expand = one_hot(el % BLOCK == er // 2 * 2 + el // LANES)
+    low8 = low[:8]
+
+    def one_row(y):
+        start = pl.multiple_of(y * 8, 8)
+        weights = jnp.concatenate(
+            [w_ref[pl.ds(start, 8), s].reshape(8 * BLOCK, LANES) for s in range(2)], axis=1
+        )
+        source = source_ref[:, pl.ds(start, 8), :].reshape(LANES, 2 * LANES).astype(bf16)
+        products = lax.dot_general(
+            weights, source, (((1,), (1,)), ((), ())), preferred_element_type=f32
+        ).reshape(8, BLOCK, LANES)
+        kept = products[0]
+        for z in range(1, 8):
+            kept = jnp.where(spot == z, products[z], kept)
+        kept = jnp.where(same_slot, kept, 0.0)
+        spread = jnp.dot(kept.T.astype(bf16), expand, preferred_element_type=f32)
+        parts = []
+        for c in range(2):
+            strips = []
+            for s in range(2):
+                total = None
+                for k in range(2):
+                    for h in range(2):
+                        at = s * 64 + k * 32 + c * 16 + h * 8
+                        term = spread[at : at + 8, h * LANES : (h + 1) * LANES]
+                        total = term if total is None else total + term
+                strips.append(total)
+            parts.append(jnp.where(low8, strips[0], strips[1]))
+        return jnp.concatenate(parts, axis=1)
+
+    def two_rows(step, carry):
+        at = pl.multiple_of(step * 16, 16)
+        warped = jnp.concatenate([one_row(step * 2), one_row(step * 2 + 1)], axis=0)
+        now = current_ref[pl.ds(at, 16), :].astype(f32)
+        out_ref[pl.ds(at, 16), :] = (now + warped).astype(bf16)
+        return carry
+
+    lax.fori_loop(0, rows // 16, two_rows, 0)
+
+
+def adjoint_kernel(w_ref, grad_ref, index_ref, out_ref, spread_ref, own_ref, other_ref):
+    f32, bf16 = jnp.float32, jnp.bfloat16
+    rows = ROWS
+    low = lax.broadcasted_iota(jnp.int32, (rows, LANES), 1) < BLOCK
+    grad = grad_ref[...].astype(bf16)
+    er = lax.broadcasted_iota(jnp.int32, (LANES, 8 * BLOCK), 0)
+    el = lax.broadcasted_iota(jnp.int32, (LANES, 8 * BLOCK), 1)
+    for s in range(2):
+        for h in range(2):
+            expand = one_hot(er == s * BLOCK + el % BLOCK // 2 * 2 + h)
+            for c in range(2):
+                spread_ref[s * 4 + c * 2 + h] = jnp.dot(
+                    grad[:, c * LANES : (c + 1) * LANES], expand, preferred_element_type=f32
+                )
+
+    mr = lax.broadcasted_iota(jnp.int32, (8, 8 * BLOCK), 0)
+    ml = lax.broadcasted_iota(jnp.int32, (8, 8 * BLOCK), 1)
+    masks = [(ml // BLOCK == mr) & (ml % 2 == k) for k in range(2)]
+    low8 = low[:8]
+
+    def one_row(y):
+        start = pl.multiple_of(y * 8, 8)
+        tiles = []
+        for s in range(2):
+            values = [spread_ref[s * 4 + ch, pl.ds(start, 8), :] for ch in range(4)]
+            left = jnp.concatenate(
+                [jnp.where(masks[k], values[ch], 0.0) for k in range(2) for ch in range(4)],
+                axis=0,
+            ).astype(bf16)
+            weights = w_ref[pl.ds(start, 8), s].reshape(8 * BLOCK, LANES)
+            tiles.append(jnp.dot(left, weights, preferred_element_type=f32))
+        for k, ref in enumerate((own_ref, other_ref)):
+            for c in range(2):
+                at = k * 32 + c * 16
+                plain = jnp.where(low8, tiles[0][at : at + 8], tiles[1][at + 8 : at + 16])
+                moved = jnp.where(low8, tiles[1][at : at + 8], tiles[0][at + 8 : at + 16])
+                ref[c, pl.ds(start, 8), :] = plain + turn(moved)
+
+    def two_rows(step, carry):
+        one_row(step * 2)
+        one_row(step * 2 + 1)
+        return carry
+
+    lax.fori_loop(0, rows // 16, two_rows, 0)
+    numbers = lax.broadcasted_iota(jnp.int32, (2 * rows, rows), 0)
+    index = index_ref[...]
+    select = jnp.concatenate(
+        [one_hot(index[s : s + 1, :] == numbers) for s in range(2)], axis=1
+    )
+    terms = jnp.concatenate(strips_to_parts(other_ref[0], other_ref[1], low), axis=0)
+    upper = terms.astype(bf16)
+    lower = (terms - upper.astype(f32)).astype(bf16)
+    summed = jnp.dot(select, upper, preferred_element_type=f32) + jnp.dot(
+        select, lower, preferred_element_type=f32
+    )
+    parts = strips_to_parts(summed[:rows], summed[rows:], low)
+    out_ref[...] = jnp.concatenate(
+        [parts[0] + own_ref[0], parts[1] + own_ref[1]], axis=1
+    ).astype(bf16)
+
+
+def band_call(kernel, bands, inputs, specs, scratch, flops, moved):
+    return pl.pallas_call(
+        kernel,
+        grid=(bands,),
+        in_specs=specs,
+        out_specs=pl.BlockSpec((ROWS, 2 * LANES), lambda b: (b, 0)),
+        out_shape=jax.ShapeDtypeStruct((bands * ROWS, 2 * LANES), jnp.bfloat16),
+        scratch_shapes=scratch,
+        compiler_params=pltpu.CompilerParams(vmem_limit_bytes=40 * 1024 * 1024),
+        cost_estimate=pl.CostEstimate(flops=flops, bytes_accessed=moved, transcendentals=0),
+    )(*inputs)
+
+
+def weight_spec():
+    return pl.BlockSpec((ROWS, 2, BLOCK, LANES), lambda b: (b, 0, 0, 0))
+
+
+def image_spec():
+    return pl.BlockSpec((ROWS, 2 * LANES), lambda b: (b, 0))
+
+
+def warp_forward(earlier, current, weights, index_columns):
+    bands = earlier.shape[0] // ROWS
+    return band_call(
+        forward_kernel,
+        bands,
+        (weights, earlier, current, index_columns),
+        [weight_spec(), image_spec(), image_spec(), pl.BlockSpec((ROWS, 2), lambda b: (b, 0))],
+        [pltpu.VMEM((16, ROWS, 2 * LANES), jnp.float32)],
+        bands * 2**31,
+        bands * 2**22,
+    )
+
+
+def warp_adjoint(grad, weights, index_rows):
+    bands = grad.shape[0] // ROWS
+    return band_call(
+        adjoint_kernel,
+        bands,
+        (weights, grad, index_rows),
+        [weight_spec(), image_spec(), pl.BlockSpec((2, ROWS), lambda b: (0, b))],
+        [
+            pltpu.VMEM((8, ROWS, 8 * BLOCK), jnp.float32),
+            pltpu.VMEM((2, ROWS, LANES), jnp.float32),
+            pltpu.VMEM((2, ROWS, LANES), jnp.float32),
+        ],
+        bands * 2**31,
+        bands * 2**22,
+    )
+
+
+def arrange_weights(blocks):
+    count = blocks.shape[0]
+    lines = blocks.reshape(count, 2, BLOCK * BLOCK // LANES, LANES)
+    return lines.transpose(0, 2, 1, 3).reshape(count // 2, 2, BLOCK, LANES)
+
+
+def band_places(block_index):
+    in_band = block_index[:, 1] % (2 * ROWS)
+    return (in_band % 2 * ROWS + in_band // 2).reshape(-1, 2)
 
 
 def on_device(cine_image, warp_blocks, warp_index, sample_mask, kspace_data, sensitivity):
@@ -120,13 +299,12 @@
     row_matrix = make_row_matrix(NX)
     column_tables = make_column_tables(NY)
     earlier = shifted(cine_image, "bin", 1)[0]
-    block_count = warp_index.shape[1]
-    local_index = warp_index[0] - lax.axis_index("coil") * block_count
-    weights = warp_blocks[0]
-    warped = join_blocks(
-        warp_forward(earlier, weights, local_index), row_count, depth_count, full_width
-    )
-    moved_image = (current.astype(jnp.float32) + warped).astype(jnp.bfloat16)
+    weights = arrange_weights(warp_blocks[0])
+    places = band_places(warp_index[0])
+    flat_shape = (row_count * depth_count, full_width)
+    moved_image = warp_forward(
+        earlier.reshape(flat_shape), current.reshape(flat_shape), weights, places
+    ).reshape(current.shape)
     measured = kspace_data[0]
     mask_now = sample_mask[0]
     coil_sens = lax.all_to_all(sensitivity, "coil", split_axis=0, concat_axis=1, tiled=True)
@@ -141,10 +319,7 @@
         scatter_dimension=0,
         tiled=True,
     ).astype(jnp.float32)
-    pieces = split_blocks(data_grad.astype(jnp.bfloat16))
-    pulled = join_blocks(
-        warp_adjoint(pieces, weights, local_index), row_count, depth_count, full_width
-    ).astype(jnp.bfloat16)
+    pulled = warp_adjoint(data_grad.reshape(flat_shape), weights, places.T).reshape(current.shape)
     from_next = shifted(pulled, "bin", -1)
     return (data_grad + from_next.astype(jnp.float32))[None]
 

time: 256 us -> 163 us (0.64)
  local copies, waits for them, and re-layouts: 127 us -> 19 us
  Pallas kernels: 0 us -> 46.5 us
  matrix products: 41.3 us -> 8.65 us
  waiting for transfers between devices: 51.6 us -> 57.4 us
    another operation x3 -> x0, local copies, waits for them, and re-layouts: 46.6 us -> none  [the longest x1 46 us: warp_forward(): matrices = weights.reshape(weights.shape[0], weights.shape[1], BLOCK, BLOCK)]
    pallas_call x0 -> x2, Pallas kernels: none -> 46.5 us  [band_call(): pl.pallas_call(kernel, grid=(bands,), in_specs=specs, out_specs=pl.BlockS...]
    unnamed x28 -> x29, local copies, waits for them, and re-layouts: 49.4 us -> 8.46 us
    dot_general x3 -> x0, matrix products: 32.5 us -> none  [the longest x1 15.8 us: warp_forward(): jnp.einsum('ikpq,ikcq->icp', matrices, chosen, preferred_element_type=jnp...]
    gather x1 -> x0, local copies, waits for them, and re-layouts: 13.8 us -> none  [warp_forward(): chosen = jnp.take(pieces, block_index, axis=0)]
    ppermute x2, waiting for transfers between devices: 3.89 us -> 10 us  [shifted(): return lax.ppermute(block, axis, route)]
    reshape x4 -> x1, local copies, waits for them, and re-layouts: 4.53 us -> 0.05 us  [on_device(): warp_adjoint(data_grad.reshape(flat_shape), weights, places.T)]
  transfers between devices with their start and end apart: 5 -> 5, of which waited for: 3 -> 4; matrix products, arithmetic and copies ran while one was open for 53% -> 7% of each run, Pallas kernels for 0% -> 19%
where the time goes in v1:
time: 163 us
  waiting for transfers between devices  57.4 us (35%)
  Pallas kernels  46.5 us (29%)
  local copies, waits for them, and re-layouts  19 us (12%)
  between operations  13.6 us (8%)
  other arithmetic  9.47 us (6%)
  matrix products  8.65 us (5%)
  starting transfers between devices  8.25 us (5%)
    pallas_call x2, Pallas kernels, band_call(): pl.pallas_call(kernel, grid=(bands,), in_specs=specs, out_specs=pl.BlockS...  46.5 us
    reduce_scatter x1, waiting for transfers between devices, on_device(): lax.psum_scatter(conj_sum(sens_rows, row_apply(back_columns, row_matrix,...  26.8 us
    all_gather x1, waiting for transfers between devices, on_device(): lax.all_gather(moved_image, 'coil', axis=0, tiled=True)  20.6 us
    ppermute x2, waiting for transfers between devices, shifted(): return lax.ppermute(block, axis, route)  10 us
    unnamed x29, local copies, waits for them, and re-layouts  8.46 us
    dot_general x2, matrix products, column_transform(): jnp.einsum('tky,cyzx->tckzx', tables, values, preferred_element_type=jnp....  7.69 us
    all_to_all x1, starting transfers between devices, on_device(): lax.all_to_all(sensitivity, 'coil', split_axis=0, concat_axis=1, tiled=True)  6.45 us
    another operation x4, other arithmetic  5.17 us
  transfers between devices with their start and end apart: 5, of which 4 were waited for; matrix products, arithmetic and copies ran while one was open for 7% of the time, Pallas kernels for 19%

profile of v1, /device:TPU:0, one launch (start us, length us, event | category | flops | bytes accessed | tf_op | source)
XLA Modules:
  0.0 162.9 jit_solution(1274659952904707552)
XLA Ops:
  6.5 6.4 %all-to-all-start = ((bf16[8,64,8,256]{3,2,1,0:T(8,128)(2,1)}), bf16[8,64,8,256]{3,2,1,0:T(8,128)(2,1)S(1)}, u32[]{:S(2)}, u32[]{:S(2)}) async-start(bf16[8,64,8,256]{3,2,1,0:T(8,128)(2,1)} %param.11), calls=%async_computation | async-start | bytes 4194304 | tf_op jit(solution)/shard_map/all_to_all | solution.py:310
  13.6 6.1 %collective-permute-done = bf16[1,64,8,256]{3,2,1,0:T(8,128)(2,1)S(1)} collective-permute-done((bf16[1,64,8,256]{3,2,1,0:T(8,128)(2,1)S(1)}, bf16[1,64,8,256]{3,2,1,0:T(8,128)(2,1)S(1)}, u32[]{:S(2)}, u32[]{:S(2)}) %collective-permute-start) | collective-permute-done | bytes 262176 | tf_op jit(solution)/shard_map/ppermute | solution.py:18
  19.7 31.6 %shard_map.64 = bf16[512,256]{1,0:T(8,128)(2,1)} custom-call(bf16[512,2,64,128]{3,2,1,0:T(8,128)(2,1)} %bitcast.94, bf16[512,256]{1,0:T(8,128)(2,1)S(1)} %bitcast.86, bf16[512,256]{1,0:T(8,128)(2,1)S(1)} %bitcast.85, s32[512,2]{1,0:T(8,128)S(1)} %copy.36.index_ref), custom_call_target="tpu_custom_call" | custom-call | flops 8589934592 | bytes 16777216 | tf_op jit(solution)/shard_map/pallas_call | solution.py:235
  51.6 4.3 %copy.41 = bf16[1,2,256,8,256]{2,4,3,1,0:T(8,128)(2,1)} copy(bf16[1,2,256,8,256]{4,3,2,1,0:T(8,128)(2,1)} %param.10) | data formatting | bytes 4194304 | tf_op args[4]
  55.9 0.9 fusion.42
  56.7 0.9 negate_convert_fusion
  57.6 1.7 %multiply_convert_fusion = (bf16[1,256,256]{2,1,0:T(8,128)(2,1)S(1)}, bf16[1,256,256]{2,1,0:T(8,128)(2,1)}) fusion(), kind=kLoop, calls=%fused_computation.53 | loop fusion | flops 1179648 | bytes 262144 | tf_op jit(solution)/shard_map/convert.4
  59.3 20.6 %all-gather.2.cloned.1.call-done = bf16[256,8,256]{2,1,0:T(8,128)(2,1)} async-done(((bf16[64,8,256]{2,1,0:T(8,128)(2,1)}), bf16[256,8,256]{2,1,0:T(8,128)(2,1)}) %all-gather.2.cloned.1.call-update) | async-done | bytes 1048592 | tf_op jit(solution)/shard_map/all_gather | solution.py:312
  80.0 1.3 slice_convert_fusion.1
  81.3 1.2 copy.37
  82.5 1.2 copy.38
  83.6 1.3 copy-done.2
  85.0 2.2 %copy.30 = bf16[4,2,64,8,256]{4,2,0,3,1:T(8,128)(2,1)S(1)} copy(bf16[4,2,64,8,256]{4,3,2,1,0:T(8,128)(2,1)} %bitcast.91) | data formatting | bytes 4194304 | tf_op jit(solution)/shard_map/all_to_all | solution.py:310
  87.2 1.7 %fusion.7 = (bf16[2,256,8,128]{3,1,2,0:T(8,128)(2,1)S(1)}, bf16[2,256,8,128]{3,1,2,0:T(8,128)(2,1)}) fusion(f32[256,8,128]{2,0,1:T(8,128)S(1)} %copy-done.4, f32[256,8,128]{2,0,1:T(8,128)S(1)} %copy-done.3, bf16[2,256,8,256]{3,1,2,0:T(8,128)(2,1)S(1)} %bitcast.89), kind=kLoop, calls=%fused_computation.21 | loop fusion | flops 5242880 | bytes 6291456 | tf_op jit(solution)/shard_map/convert.11
  88.9 6.3 %convolution_bitcast_fusion.1 = f32[2,2,256,8,256]{2,4,0,3,1:T(8,128)} fusion(bf16[2,256,8,128]{3,1,2,0:T(8,128)(2,1)} %get-tuple-element.12, bf16[2,256,8,128]{3,1,2,0:T(8,128)(2,1)S(1)} %get-tuple-element.11, bf16[1,256,256]{2,1,0:T(8,128)(2,1)S(1)} %get-tuple-element.15, bf16[1,256,256]{2,1,0:T(8,128)(2,1)} %get-tuple-element.16, ...), kind=kOutput, calls=%fused_computation.19 | convolution fusion | flops 1616904192 | bytes 10846208 | tf_op jit(solution)/shard_map/tky,cyzx->tckzx/dot_general | solution.py:48
  95.2 2.7 %slice_bitcast_fusion.2 = f32[2,256,8,256]{1,3,2,0:T(8,128)S(1)} fusion(f32[2,2,256,8,256]{2,4,0,3,1:T(8,128)} %convolution_bitcast_fusion.1), kind=kLoop, calls=%fused_computation.4 | loop fusion | bytes 8388608 | tf_op jit(solution)/shard_map/squeeze | solution.py:49
  98.0 0.4 fusion.52
  98.7 1.7 %slice-done.1 = s8[4194304]{0:T(1024)(128)(4,1)S(1)} async-done(((s8[8388608]{0:T(1024)(128)(4,1)}), s8[4194304]{0:T(1024)(128)(4,1)S(1)}, s32[]{:S(2)}) %slice-start.1) | async-done | bytes 4194328
  100.4 0.6 copy-done.1
  101.0 1.4 convolution_bitcast_fusion
  102.3 0.4 slice_bitcast_fusion
  102.7 0.4 slice_negate_fusion
  103.2 0.3 copy-done.7
  103.5 1.0 fusion.16
  104.5 0.8 fusion.11
  105.3 1.1 pad_maximum_fusion
  106.5 26.8 %reduce-scatter.2.cloned.1.call-done = bf16[64,8,256]{2,0,1:T(8,128)(2,1)} async-done(((bf16[256,8,256]{2,0,1:T(8,128)(2,1)}), bf16[64,8,256]{2,0,1:T(8,128)(2,1)}) %reduce-scatter.2.cloned.1.call-update) | async-done | bytes 262160 | tf_op jit(solution)/shard_map/reduce_scatter | solution.py:316
  133.2 1.1 copy.57
  134.4 14.9 %shard_map.65 = bf16[512,256]{1,0:T(8,128)(2,1)S(1)} custom-call(bf16[512,2,64,128]{3,2,1,0:T(8,128)(2,1)} %bitcast.95, f32[512,256]{1,0:T(8,128)S(1)} %bitcast.83, s32[2,512]{1,0:T(2,128)S(1)} %fusion.53.index_ref), custom_call_target="tpu_custom_call" | custom-call | flops 8589934592 | bytes 16777216 | tf_op jit(solution)/shard_map/pallas_call | solution.py:235
  149.3 1.7 %collective-permute-start.1 = (bf16[64,8,256]{2,0,1:T(8,128)(2,1)S(1)}, bf16[64,8,256]{2,0,1:T(8,128)(2,1)S(1)}, u32[]{:S(2)}, u32[]{:S(2)}) collective-permute-start(bf16[64,8,256]{2,0,1:T(8,128)(2,1)S(1)} %copy.45), channel_id=1, source_target_pairs={{4,0},{8,4},{12,8},{16,12},{20,16},{24,20},{28,24},{0,28},{5,1},{9... | collective-permute-start | bytes 786440 | tf_op jit(solution)/shard_map/ppermute | solution.py:18
  151.0 3.9 %collective-permute-done.1 = bf16[64,8,256]{2,0,1:T(8,128)(2,1)S(1)} collective-permute-done((bf16[64,8,256]{2,0,1:T(8,128)(2,1)S(1)}, bf16[64,8,256]{2,0,1:T(8,128)(2,1)S(1)}, u32[]{:S(2)}, u32[]{:S(2)}) %collective-permute-start.1) | collective-permute-done | bytes 262176 | tf_op jit(solution)/shard_map/ppermute | solution.py:18
  155.0 1.1 copy.46
  (41 shorter events, 1.2 us)
Async XLA Ops:
  6.5 6.5 %copy-start = (bf16[1,64,8,256]{3,2,1,0:T(8,128)(2,1)S(1)}, bf16[1,64,8,256]{3,2,1,0:T(8,128)(2,1)}, u32[]{:S(2)}) copy-start(bf16[1,64,8,256]{3,2,1,0:T(8,128)(2,1)} %param.6) | copy-start | bytes 786436
  6.5 6.5 %copy-start.11 = (s32[1,1024,2]{1,2,0:T(2,128)S(1)}, s32[1,1024,2]{1,2,0:T(2,128)}, u32[]{:S(2)}) copy-start(s32[1,1024,2]{1,2,0:T(2,128)} %param.8) | copy-start | bytes 24580
  6.5 77.1 %all-to-all-start = ((bf16[8,64,8,256]{3,2,1,0:T(8,128)(2,1)}), bf16[8,64,8,256]{3,2,1,0:T(8,128)(2,1)S(1)}, u32[]{:S(2)}, u32[]{:S(2)}) async-start(bf16[8,64,8,256]{3,2,1,0:T(8,128)(2,1)} %param.11), calls=%async_computation | async-start | bytes 4194304 | tf_op jit(solution)/shard_map/all_to_all | solution.py:310
  13.0 67.0 %all-gather.2.cloned.1.call-start = ((), (), s32[]{:S(2)}) async-start(), calls=%async_computation.2 | async-start | bytes 1310720 | tf_op jit(solution)/shard_map/all_gather | solution.py:312
  13.0 6.7 %collective-permute-start = (bf16[1,64,8,256]{3,2,1,0:T(8,128)(2,1)S(1)}, bf16[1,64,8,256]{3,2,1,0:T(8,128)(2,1)S(1)}, u32[]{:S(2)}, u32[]{:S(2)}) collective-permute-start(bf16[1,64,8,256]{3,2,1,0:T(8,128)(2,1)S(1)} %copy-done), channel_id=1, source_target_pairs={{28,0},{0,4},{4,8},{8,12},{12,16},{16,20},{20,24},{24,28},{29,1},{... | collective-permute-start | bytes 786440 | tf_op jit(solution)/shard_map/ppermute | solution.py:18
  19.7 31.7 %copy-start.10 = (s32[1,256,128]{2,1,0:T(8,128)S(1)}, s32[1,256,128]{2,1,0:T(8,128)}, u32[]{:S(2)}) copy-start(s32[1,256,128]{2,1,0:T(8,128)} %param.9) | copy-start | bytes 393220
  51.3 81.9 %reduce-scatter.2.cloned.1.call-start = ((), (), s32[]{:S(2)}) async-start(), calls=%async_computation.3 | async-start | bytes 1310720 | tf_op jit(solution)/shard_map/reduce_scatter | solution.py:316
  83.6 1.3 copy-start.2
  85.0 2.2 %copy-start.3 = (f32[256,8,128]{2,0,1:T(8,128)S(1)}, f32[256,8,128]{2,0,1:T(8,128)}, u32[]{:S(2)}) copy-start(f32[256,8,128]{2,0,1:T(8,128)} %copy.37) | copy-start | bytes 3145732
  85.0 2.3 %copy-start.4 = (f32[256,8,128]{2,0,1:T(8,128)S(1)}, f32[256,8,128]{2,0,1:T(8,128)}, u32[]{:S(2)}) copy-start(f32[256,8,128]{2,0,1:T(8,128)} %copy.38) | copy-start | bytes 3145732
  95.2 3.5 %slice-start = ((s8[8388608]{0:T(1024)(128)(4,1)}), s8[4194304]{0:T(1024)(128)(4,1)S(1)}, s32[]{:S(2)}) async-start(s8[8388608]{0:T(1024)(128)(4,1)} %bitcast.87), calls=%async_computation.4 | async-start | bytes 8388608
  98.0 2.4 %slice-start.1 = ((s8[8388608]{0:T(1024)(128)(4,1)}), s8[4194304]{0:T(1024)(128)(4,1)S(1)}, s32[]{:S(2)}) async-start(s8[8388608]{0:T(1024)(128)(4,1)} %bitcast.87), calls=%async_computation.5 | async-start | bytes 8388608
  98.0 2.9 %copy-start.1 = (bf16[1,2,256,8,256]{2,4,3,1,0:T(8,128)(2,1)S(1)}, bf16[1,2,256,8,256]{2,4,3,1,0:T(8,128)(2,1)}, u32[]{:S(2)}) copy-start(bf16[1,2,256,8,256]{2,4,3,1,0:T(8,128)(2,1)} %copy.41) | copy-start | bytes 6291460
  98.0 2.9 %copy-start.5 = (bf16[1,256,256]{2,1,0:T(8,128)(2,1)S(1)}, bf16[1,256,256]{2,1,0:T(8,128)(2,1)}, u32[]{:S(2)}) copy-start(bf16[1,256,256]{2,1,0:T(8,128)(2,1)} %get-tuple-element.16) | copy-start | bytes 393220
  102.7 0.8 copy-start.7
  102.7 0.8 copy-start.8
  102.7 0.8 copy-start.9
  134.4 20.5 %copy-start.6 = (bf16[64,8,256]{2,0,1:T(8,128)(2,1)S(1)}, bf16[64,8,256]{2,0,1:T(8,128)(2,1)}, u32[]{:S(2)}) copy-start(bf16[64,8,256]{2,0,1:T(8,128)(2,1)} %reduce-scatter.2.cloned.1.call-done) | copy-start | bytes 786436
  149.3 5.6 %collective-permute-start.1 = (bf16[64,8,256]{2,0,1:T(8,128)(2,1)S(1)}, bf16[64,8,256]{2,0,1:T(8,128)(2,1)S(1)}, u32[]{:S(2)}, u32[]{:S(2)}) collective-permute-start(bf16[64,8,256]{2,0,1:T(8,128)(2,1)S(1)} %copy.45), channel_id=1, source_target_pairs={{4,0},{8,4},{12,8},{16,12},{20,16},{24,20},{28,24},{0,28},{5,1},{9... | collective-permute-start | bytes 786440 | tf_op jit(solution)/shard_map/ppermute | solution.py:18
Sparse Core Ops, SparseCore 0:
  51.5 28.4 all-gather.1
  106.6 26.6 reduce-scatter.1

commit v2 on v1

--- a/solution.py
+++ b/solution.py
@@ -38,50 +38,131 @@
     return jnp.stack([cosine_table, sine_table]).astype(jnp.bfloat16)
 
 
-def row_apply(values, row_matrix, inverse):
-    flattened = values.reshape(-1, values.shape[-1])
-    table_used = row_matrix.T if inverse else row_matrix
-    return jnp.dot(flattened, table_used, preferred_element_type=jnp.float32).reshape(values.shape)
-
-
-def column_transform(values, tables, inverse):
-    products = jnp.einsum("tky,cyzx->tckzx", tables, values, preferred_element_type=jnp.float32)
-    direct, turned = (products[0], products[1])
-    half_width = direct.shape[-1] // 2
-    if inverse:
-        swapped = jnp.concatenate([-turned[..., half_width:], turned[..., :half_width]], axis=-1)
-    else:
-        swapped = jnp.concatenate([turned[..., half_width:], -turned[..., :half_width]], axis=-1)
-    return direct + swapped
-
-
-def coil_images(sensitivity, moved_image):
-    half_width = moved_image.shape[-1] // 2
-    sens_re = sensitivity[..., :half_width].astype(jnp.float32)
-    sens_im = sensitivity[..., half_width:].astype(jnp.float32)
-    image_re = moved_image[..., :half_width].astype(jnp.float32)
-    image_im = moved_image[..., half_width:].astype(jnp.float32)
-    real_part = sens_re * image_re - sens_im * image_im
-    imag_part = sens_re * image_im + sens_im * image_re
-    return jnp.concatenate([real_part, imag_part], axis=-1).astype(jnp.bfloat16)
-
-
-def conj_sum(sensitivity, back_rows):
-    half_width = back_rows.shape[-1] // 2
-    sens_re = sensitivity[..., :half_width].astype(jnp.float32)
-    sens_im = sensitivity[..., half_width:].astype(jnp.float32)
-    back_re = back_rows[..., :half_width]
-    back_im = back_rows[..., half_width:]
-    real_part = jnp.sum(sens_re * back_re + sens_im * back_im, axis=0)
-    imag_part = jnp.sum(sens_re * back_im - sens_im * back_re, axis=0)
-    return jnp.concatenate([real_part, imag_part], axis=-1)
-
-
-def column_part(row_spectra, measured, mask_now, column_tables):
-    spectra = column_transform(row_spectra, column_tables, False)
-    weight_mask = jnp.concatenate([mask_now, mask_now], axis=1).astype(jnp.float32)[:, None, :]
-    residual = (weight_mask * (spectra - measured.astype(jnp.float32))).astype(jnp.bfloat16)
-    return column_transform(residual, column_tables, True).astype(jnp.bfloat16)
+def halves_swapped(values):
+    return jnp.concatenate([values[:, LANES:], values[:, :LANES]], axis=1)
+
+
+def coil_kernel(
+    moved_ref, sens_ref, kspace_ref, mask_ref, row_ref, back_ref, column_ref, out_ref,
+    wide_ref, sums_ref, send_ref, recv_ref, send_sem, recv_sem,
+):
+    f32, bf16 = jnp.float32, jnp.bfloat16
+    me, count = lax.axis_index("coil"), lax.axis_size("coil")
+    coils, depth = sens_ref.shape[0], sens_ref.shape[1]
+    own = NY // count
+    meet("coil")
+    for part in range(2):
+        wide_ref[part] = moved_ref[:, part * LANES : (part + 1) * LANES].astype(f32)
+
+    def multiply(left, right):
+        return jnp.dot(left, right, preferred_element_type=f32)
+
+    def transfer(step, z):
+        target = lax.rem(me + step, count)
+        rows = pl.ds(pl.multiple_of(target * own, own), own)
+        return pltpu.make_async_remote_copy(
+            src_ref=send_ref.at[z, rows],
+            dst_ref=recv_ref.at[step - 1, z],
+            send_sem=send_sem.at[step - 1, z],
+            recv_sem=recv_sem.at[step - 1, z],
+            device_id={"coil": target},
+            device_id_type=pl.DeviceIdType.MESH,
+        )
+
+    def one_depth(z, carry):
+        image_re = wide_ref[0, pl.ds(z, NY, stride=depth), :]
+        image_im = wide_ref[1, pl.ds(z, NY, stride=depth), :]
+        mask = mask_ref[...].astype(f32)
+        mask = jnp.concatenate([mask, mask], axis=1)
+        total_re = total_im = 0.0
+        for c in range(coils):
+            sens = sens_ref[c, z].astype(f32)
+            sens_re, sens_im = sens[:, :LANES], sens[:, LANES:]
+            coil_image = jnp.concatenate(
+                [
+                    sens_re * image_re - sens_im * image_im,
+                    sens_re * image_im + sens_im * image_re,
+                ],
+                axis=1,
+            ).astype(bf16)
+            row_spectra = multiply(coil_image, row_ref[...]).astype(bf16)
+            products = multiply(column_ref[...], row_spectra)
+            direct, turned = products[:NY], halves_swapped(products[NY:])
+            spectra = jnp.concatenate(
+                [direct[:, :LANES] + turned[:, :LANES], direct[:, LANES:] - turned[:, LANES:]],
+                axis=1,
+            )
+            residual = (mask * (spectra - kspace_ref[c, z].astype(f32))).astype(bf16)
+            products = multiply(column_ref[...], residual)
+            direct, turned = products[:NY], halves_swapped(products[NY:])
+            columns = jnp.concatenate(
+                [direct[:, :LANES] - turned[:, :LANES], direct[:, LANES:] + turned[:, LANES:]],
+                axis=1,
+            ).astype(bf16)
+            back = multiply(columns, back_ref[...])
+            back_re, back_im = back[:, :LANES], back[:, LANES:]
+            total_re += sens_re * back_re + sens_im * back_im
+            total_im += sens_re * back_im - sens_im * back_re
+        send_ref[z] = jnp.concatenate([total_re, total_im], axis=1).astype(bf16)
+        for step in range(1, count):
+            transfer(step, z).start()
+        return carry
+
+    def collect(z, carry):
+        rows = pl.ds(pl.multiple_of(me * own, own), own)
+        total = send_ref[z, rows, :].astype(f32)
+        for step in range(1, count):
+            transfer(step, z).wait_recv()
+            total += recv_ref[step - 1, z].astype(f32)
+        for part in range(2):
+            sums_ref[part, pl.ds(z, own, stride=depth), :] = total[
+                :, part * LANES : (part + 1) * LANES
+            ]
+        for step in range(1, count):
+            transfer(step, z).wait_send()
+        return carry
+
+    lax.fori_loop(0, depth, one_depth, 0)
+    lax.fori_loop(0, depth, collect, 0)
+    out_ref[...] = jnp.concatenate([sums_ref[0], sums_ref[1]], axis=1)
+
+
+def coil_gradient(moved, sens, kspace, mask, row_matrix, column_tables):
+    count = lax.axis_size("coil")
+    coils, depth = sens.shape[:2]
+    own = NY // count
+    vmem = pl.BlockSpec(memory_space=pltpu.VMEM)
+    return pl.pallas_call(
+        coil_kernel,
+        in_specs=[vmem] * 7,
+        out_specs=vmem,
+        out_shape=jax.ShapeDtypeStruct((own * depth, 2 * LANES), jnp.float32),
+        scratch_shapes=[
+            pltpu.VMEM((2, NY * depth, LANES), jnp.float32),
+            pltpu.VMEM((2, own * depth, LANES), jnp.float32),
+            pltpu.VMEM((depth, NY, 2 * LANES), jnp.bfloat16),
+            pltpu.VMEM((count - 1, depth, own, 2 * LANES), jnp.bfloat16),
+            pltpu.SemaphoreType.DMA((count - 1, depth)),
+            pltpu.SemaphoreType.DMA((count - 1, depth)),
+        ],
+        compiler_params=pltpu.CompilerParams(
+            collective_id=1, has_side_effects=True, vmem_limit_bytes=40 * 1024 * 1024
+        ),
+        cost_estimate=pl.CostEstimate(
+            flops=coils * 2**31, bytes_accessed=coils * 2**22, transcendentals=0
+        ),
+    )(moved, sens, kspace, mask, row_matrix, row_matrix.T, column_tables)
+
+
+def own_coil_maps(sensitivity):
+    coils, row_count, depth, width = sensitivity.shape
+    bins, count = lax.axis_size("bin"), lax.axis_size("coil")
+    share = row_count // bins
+    mine = lax.dynamic_slice_in_dim(sensitivity, lax.axis_index("bin") * share, share, axis=1)
+    swapped = lax.all_to_all(mine, "coil", split_axis=0, concat_axis=1, tiled=True)
+    full = lax.all_gather(swapped, "bin", axis=0, tiled=False)
+    full = full.reshape(bins, coils // count, count, share, depth, width)
+    return full.transpose(1, 4, 2, 0, 3, 5).reshape(coils // count, depth, NY, width)
 
 
 def one_hot(test):
@@ -96,7 +177,66 @@
     return jnp.where(low, first, turn(second)), jnp.where(low, turn(first), second)
 
 
-def forward_kernel(w_ref, earlier_ref, current_ref, index_ref, out_ref, source_ref):
+def meet(axis):
+    me, count = lax.axis_index(axis), lax.axis_size(axis)
+    barrier = pltpu.get_barrier_semaphore()
+    for step in range(1, count):
+        pl.semaphore_signal(
+            barrier,
+            inc=1,
+            device_id={axis: lax.rem(me + step, count)},
+            device_id_type=pl.DeviceIdType.MESH,
+        )
+    pl.semaphore_wait(barrier, count - 1)
+
+
+def forward_kernel(
+    w_hbm, earlier_ref, current_ref, index_ref, out_ref, w_buffer, source_ref,
+    load_sem, send_sem, recv_sem,
+):
+    me, count = lax.axis_index("coil"), lax.axis_size("coil")
+    total_rows = current_ref.shape[0]
+    bands = total_rows // ROWS
+    first_row = me * total_rows
+
+    def load(b):
+        return pltpu.make_async_copy(
+            w_hbm.at[pl.ds(b * ROWS, ROWS)], w_buffer.at[b % 2], load_sem.at[b % 2]
+        )
+
+    load(0).start()
+    meet("coil")
+    sends = []
+    for b in range(bands):
+        load(b).wait()
+        if b + 1 < bands:
+            load(b + 1).start()
+        part = pl.ds(b * ROWS, ROWS)
+        place = pl.ds(pl.multiple_of(first_row + b * ROWS, ROWS), ROWS)
+        forward_band(
+            w_buffer.at[b % 2],
+            earlier_ref.at[part],
+            current_ref.at[part],
+            index_ref.at[part],
+            out_ref.at[place],
+            source_ref,
+        )
+        for step in range(1, count):
+            copy = pltpu.make_async_remote_copy(
+                src_ref=out_ref.at[place],
+                dst_ref=out_ref.at[place],
+                send_sem=send_sem.at[b, step - 1],
+                recv_sem=recv_sem.at[b, step - 1],
+                device_id={"coil": lax.rem(me + step, count)},
+                device_id_type=pl.DeviceIdType.MESH,
+            )
+            copy.start()
+            sends.append(copy)
+    for copy in sends:
+        copy.wait()
+
+
+def forward_band(w_ref, earlier_ref, current_ref, index_ref, out_ref, source_ref):
     f32, bf16 = jnp.float32, jnp.bfloat16
     rows = ROWS
     low = lax.broadcasted_iota(jnp.int32, (rows, LANES), 1) < BLOCK
@@ -114,18 +254,18 @@
         for c in range(2):
             plain, turned = image[c], turn(image[c])
             zero = jnp.zeros_like(plain)
-            base = k * 4 + c * 2
+            base = k * 8 + c * 2
             source_ref[base, :, :LANES] = jnp.where(low, plain, 0.0)
             source_ref[base + 1, :, :LANES] = jnp.where(low, 0.0, turned)
-            source_ref[base + 8, :, LANES:] = jnp.where(low, turned, 0.0)
-            source_ref[base + 9, :, LANES:] = jnp.where(low, 0.0, plain)
+            source_ref[base + 4, :, LANES:] = jnp.where(low, turned, 0.0)
+            source_ref[base + 5, :, LANES:] = jnp.where(low, 0.0, plain)
             for h in range(2):
                 source_ref[base + h, :, LANES:] = zero
-                source_ref[base + 8 + h, :, :LANES] = zero
+                source_ref[base + 4 + h, :, :LANES] = zero
 
     lane = lax.broadcasted_iota(jnp.int32, (BLOCK, LANES), 1)
     row = lax.broadcasted_iota(jnp.int32, (BLOCK, LANES), 0)
-    same_slot = row % 2 == lane // 32 % 2
+    same_slot = row % 2 == lane // 64
     spot = lane % 8
     er = lax.broadcasted_iota(jnp.int32, (BLOCK, 2 * LANES), 0)
     el = lax.broadcasted_iota(jnp.int32, (BLOCK, 2 * LANES), 1)
@@ -145,29 +285,32 @@
         for z in range(1, 8):
             kept = jnp.where(spot == z, products[z], kept)
         kept = jnp.where(same_slot, kept, 0.0)
-        spread = jnp.dot(kept.T.astype(bf16), expand, preferred_element_type=f32)
-        parts = []
-        for c in range(2):
-            strips = []
-            for s in range(2):
-                total = None
-                for k in range(2):
-                    for h in range(2):
-                        at = s * 64 + k * 32 + c * 16 + h * 8
-                        term = spread[at : at + 8, h * LANES : (h + 1) * LANES]
-                        total = term if total is None else total + term
-                strips.append(total)
-            parts.append(jnp.where(low8, strips[0], strips[1]))
-        return jnp.concatenate(parts, axis=1)
-
-    def two_rows(step, carry):
+        return kept + turn(kept)
+
+    def two_rows(step):
         at = pl.multiple_of(step * 16, 16)
-        warped = jnp.concatenate([one_row(step * 2), one_row(step * 2 + 1)], axis=0)
+        pair = jnp.where(lane < BLOCK, one_row(step * 2), one_row(step * 2 + 1))
+        spread = jnp.dot(pair.T.astype(bf16), expand, preferred_element_type=f32)
+        lines = []
+        for y in range(2):
+            parts = []
+            for c in range(2):
+                strips = []
+                for s in range(2):
+                    i = y * 64 + s * 32 + c * 16
+                    strips.append(spread[i : i + 8, :LANES] + spread[i + 8 : i + 16, LANES:])
+                parts.append(jnp.where(low8, strips[0], strips[1]))
+            lines.append(jnp.concatenate(parts, axis=1))
+        warped = jnp.concatenate(lines, axis=0)
         now = current_ref[pl.ds(at, 16), :].astype(f32)
         out_ref[pl.ds(at, 16), :] = (now + warped).astype(bf16)
+
+    def four_rows(step, carry):
+        two_rows(step * 2)
+        two_rows(step * 2 + 1)
         return carry
 
-    lax.fori_loop(0, rows // 16, two_rows, 0)
+    lax.fori_loop(0, rows // 32, four_rows, 0)
 
 
 def adjoint_kernel(w_ref, grad_ref, index_ref, out_ref, spread_ref, own_ref, other_ref):
@@ -253,16 +396,29 @@
 
 
 def warp_forward(earlier, current, weights, index_columns):
-    bands = earlier.shape[0] // ROWS
-    return band_call(
+    count = lax.axis_size("coil")
+    rows = earlier.shape[0]
+    bands = rows // ROWS
+    vmem = pl.BlockSpec(memory_space=pltpu.VMEM)
+    return pl.pallas_call(
         forward_kernel,
-        bands,
-        (weights, earlier, current, index_columns),
-        [weight_spec(), image_spec(), image_spec(), pl.BlockSpec((ROWS, 2), lambda b: (b, 0))],
-        [pltpu.VMEM((16, ROWS, 2 * LANES), jnp.float32)],
-        bands * 2**31,
-        bands * 2**22,
-    )
+        in_specs=[pl.BlockSpec(memory_space=pl.ANY), vmem, vmem, vmem],
+        out_specs=vmem,
+        out_shape=jax.ShapeDtypeStruct((count * rows, 2 * LANES), jnp.bfloat16),
+        scratch_shapes=[
+            pltpu.VMEM((2, ROWS, 2, BLOCK, LANES), jnp.bfloat16),
+            pltpu.VMEM((16, ROWS, 2 * LANES), jnp.float32),
+            pltpu.SemaphoreType.DMA((2,)),
+            pltpu.SemaphoreType.DMA((bands, count - 1)),
+            pltpu.SemaphoreType.DMA((bands, count - 1)),
+        ],
+        compiler_params=pltpu.CompilerParams(
+            collective_id=0, has_side_effects=True, vmem_limit_bytes=40 * 1024 * 1024
+        ),
+        cost_estimate=pl.CostEstimate(
+            flops=bands * 2**31, bytes_accessed=bands * 2**22, transcendentals=0
+        ),
+    )(weights, earlier, current, index_columns)
 
 
 def warp_adjoint(grad, weights, index_rows):
@@ -297,31 +453,22 @@
     current = cine_image[0]
     row_count, depth_count, full_width = current.shape
     row_matrix = make_row_matrix(NX)
-    column_tables = make_column_tables(NY)
+    column_tables = make_column_tables(NY).reshape(2 * NY, NY)
     earlier = shifted(cine_image, "bin", 1)[0]
+    sens = own_coil_maps(sensitivity)
+    kspace = kspace_data[0].transpose(0, 2, 1, 3)
     weights = arrange_weights(warp_blocks[0])
     places = band_places(warp_index[0])
     flat_shape = (row_count * depth_count, full_width)
     moved_image = warp_forward(
         earlier.reshape(flat_shape), current.reshape(flat_shape), weights, places
-    ).reshape(current.shape)
-    measured = kspace_data[0]
-    mask_now = sample_mask[0]
-    coil_sens = lax.all_to_all(sensitivity, "coil", split_axis=0, concat_axis=1, tiled=True)
-    sens_rows = coil_sens
-    images = coil_images(sens_rows, lax.all_gather(moved_image, "coil", axis=0, tiled=True))
-    own_coils = row_apply(images, row_matrix, False).astype(jnp.bfloat16)
-    back_columns = column_part(own_coils, measured, mask_now, column_tables)
-    sens_rows = coil_sens
-    data_grad = lax.psum_scatter(
-        conj_sum(sens_rows, row_apply(back_columns, row_matrix, True)).astype(jnp.bfloat16),
-        "coil",
-        scatter_dimension=0,
-        tiled=True,
-    ).astype(jnp.float32)
-    pulled = warp_adjoint(data_grad.reshape(flat_shape), weights, places.T).reshape(current.shape)
+    )
+    data_grad = coil_gradient(
+        moved_image, sens, kspace, sample_mask[0], row_matrix, column_tables
+    )
+    pulled = warp_adjoint(data_grad, weights, places.T).reshape(current.shape)
     from_next = shifted(pulled, "bin", -1)
-    return (data_grad + from_next.astype(jnp.float32))[None]
+    return (data_grad.reshape(current.shape) + from_next.astype(jnp.float32))[None]
 
 
 def solution(mesh):

time: 163 us -> 121 us (0.74)
  waiting for transfers between devices: 57.4 us -> 4.26 us
  Pallas kernels: 46.5 us -> 73.8 us
  blocking collectives: 0 us -> 15 us
  matrix products: 8.65 us -> 0 us
  local copies, waits for them, and re-layouts: 19 us -> 10.5 us
  starting transfers between devices: 8.25 us -> 1.19 us
  other arithmetic: 9.47 us -> 2.62 us
    pallas_call x0 -> x2, Pallas kernels: none -> 58.9 us  [the longest x1 30 us: warp_forward(): pl.pallas_call(forward_kernel, in_specs=[pl.BlockSpec(memory_space=pl.ANY...]
    pallas_call x2 -> x1, Pallas kernels: 46.5 us -> 14.8 us  [band_call(): pl.pallas_call(kernel, grid=(bands,), in_specs=specs, out_specs=pl.BlockS...]
    reduce_scatter x1 -> x0, waiting for transfers between devices: 26.8 us -> none  [on_device(): lax.psum_scatter(conj_sum(sens_rows, row_apply(back_columns, row_matrix,...]
    all_gather x1, waiting for transfers between devices: 20.6 us -> 0.01 us  [own_coil_maps(): full = lax.all_gather(swapped, 'bin', axis=0, tiled=False)]
    all_to_all x0 -> x1, blocking collectives: none -> 15 us  [own_coil_maps(): lax.all_to_all(mine, 'coil', split_axis=0, concat_axis=1, tiled=True)]
    dot_general x3 -> x0, matrix products: 8.65 us -> none  [the longest x2 7.69 us: column_transform(): jnp.einsum('tky,cyzx->tckzx', tables, values, preferred_element_type=jnp....]
    all_to_all x1 -> x0, starting transfers between devices: 6.45 us -> none  [on_device(): lax.all_to_all(sensitivity, 'coil', split_axis=0, concat_axis=1, tiled=True)]
    ppermute x2, waiting for transfers between devices: 10 us -> 4.25 us  [shifted(): return lax.ppermute(block, axis, route)]
  transfers between devices with their start and end apart: 5 -> 3, of which waited for: 4 -> 2; matrix products, arithmetic and copies ran while one was open for 7% -> 5% of each run, Pallas kernels for 19% -> 25%
where the time goes in v2:
time: 121 us
  Pallas kernels  73.8 us (61%)
  blocking collectives  15 us (12%)
  between operations  13.5 us (11%)
  local copies, waits for them, and re-layouts  10.5 us (9%)
  waiting for transfers between devices  4.26 us (4%)
  other arithmetic  2.62 us (2%)
    pallas_call x1, Pallas kernels, warp_forward(): pl.pallas_call(forward_kernel, in_specs=[pl.BlockSpec(memory_space=pl.ANY...  30 us
    pallas_call x1, Pallas kernels, coil_gradient(): pl.pallas_call(coil_kernel, in_specs=[vmem] * 7, out_specs=vmem, out_shap...  28.9 us
    all_to_all x1, blocking collectives, own_coil_maps(): lax.all_to_all(mine, 'coil', split_axis=0, concat_axis=1, tiled=True)  15 us
    pallas_call x1, Pallas kernels, band_call(): pl.pallas_call(kernel, grid=(bands,), in_specs=specs, out_specs=pl.BlockS...  14.8 us
    unnamed x13, local copies, waits for them, and re-layouts  6.24 us
    ppermute x2, waiting for transfers between devices, shifted(): return lax.ppermute(block, axis, route)  4.25 us
  transfers between devices with their start and end apart: 3, of which 2 were waited for; matrix products, arithmetic and copies ran while one was open for 5% of the time, Pallas kernels for 25%

profile of v2, /device:TPU:0, one launch (start us, length us, event | category | flops | bytes accessed | tf_op | source)
XLA Modules:
  0.0 120.8 jit_solution(10385629154189586316)
XLA Ops:
  6.5 0.0 copy-start
  6.5 0.0 all-gather.2.cloned.1.call-start
  6.5 1.6 %copy-done = bf16[8,64,8,256]{3,2,1,0:T(8,128)(2,1)S(1)} copy-done((bf16[8,64,8,256]{3,2,1,0:T(8,128)(2,1)S(1)}, bf16[8,64,8,256]{3,2,1,0:T(8,128)(2,1)}, u32[]{:S(2)}) %copy-start) | copy-done | bytes 2097176
  8.1 15.0 %all_to_all.15 = bf16[8,8,8,256]{3,2,1,0:T(8,128)(2,1)S(1)} all-to-all(bf16[8,8,8,256]{3,2,1,0:T(8,128)(2,1)S(1)} %constant_dynamic-slice_fusion), channel_id=1, replica_groups=mesh['bin'=8,'coil'=4] {'coil'}, dimensions={0} | all-to-all | bytes 524288 | tf_op jit(solution)/shard_map/all_to_all | solution.py:162
  23.1 0.7 copy.33
  23.9 0.0 all-gather.2.cloned.1.call-update
  23.9 0.1 collective-permute-start
  24.0 0.7 slice_reduce_fusion
  24.7 0.2 squeeze.13
  24.9 0.1 copy.29
  25.0 0.3 fusion.13
  25.3 0.3 negate_convert_fusion
  25.6 1.1 multiply_convert_fusion
  26.8 0.1 copy.36.row_ref
  26.9 0.1 copy.32.index_ref
  27.0 0.0 copy-start.2
  27.0 3.4 %copy.38 = bf16[1,2,256,8,256]{4,2,3,1,0:T(8,128)(2,1)} copy(bf16[1,2,256,8,256]{4,3,2,1,0:T(8,128)(2,1)} %param.10) | data formatting | bytes 4194304 | tf_op args[4]
  30.5 0.4 collective-permute-done
  30.8 0.0 copy-done.2
  30.8 30.0 %shard_map.64.moved_ref = bf16[2048,256]{1,0:T(8,128)(2,1)S(1)} custom-call(bf16[512,2,64,128]{3,2,1,0:T(8,128)(2,1)} %bitcast.45, bf16[512,256]{1,0:T(8,128)(2,1)S(1)} %bitcast.38, bf16[512,256]{1,0:T(8,128)(2,1)S(1)} %bitcast.37, s32[512,2]{1,0:T(8,128)S(1)} %copy.32.index_ref), custom_call_target="tpu_custom_call" | custom-call | flops 8589934592 | bytes 16777216 | tf_op jit(solution)/shard_map/pallas_call | solution.py:403
  60.9 0.0 copy-start.4
  60.9 1.0 copy-done.4
  61.8 0.0 all-gather.2.cloned.1.call-done
  61.9 2.2 %copy.34 = bf16[2,8,4,8,8,256]{5,4,3,2,1,0:T(8,128)(2,1)S(1)} copy(bf16[2,8,4,8,8,256]{5,1,4,2,0,3:T(8,128)(2,1)} %bitcast.41) | data formatting | bytes 4194304 | tf_op jit(solution)/shard_map/transpose | solution.py:165
  64.1 0.0 copy-done.1
  64.1 0.0 copy-done.3
  64.1 0.3 copy-done.5
  64.4 28.9 %shard_map.65.grad_ref = f32[512,256]{1,0:T(8,128)S(1)} custom-call(bf16[2048,256]{1,0:T(8,128)(2,1)S(1)} %copy-done.5, bf16[2,8,256,256]{3,2,1,0:T(8,128)(2,1)S(1)} %bitcast.35, bf16[2,8,256,256]{3,2,1,0:T(8,128)(2,1)S(1)} %bitcast.34, s32[256,128]{1,0:T(8,128)S(1)} %bitcast.40, bf16[256,256]{1,0:T(8,128)(2,1)S(1)} %copy.36.row_ref, ...), custom_call_target="tpu_custom_call" | custom-call | flops 4294967296 | bytes 8388608 | tf_op jit(solution)/shard_map/pallas_call | solution.py:135
  93.3 14.8 %shard_map.66 = bf16[512,256]{1,0:T(8,128)(2,1)S(1)} custom-call(bf16[512,2,64,128]{3,2,1,0:T(8,128)(2,1)} %bitcast.46, f32[512,256]{1,0:T(8,128)S(1)} %shard_map.65.grad_ref, s32[2,512]{1,0:T(2,128)S(1)} %fusion.18.index_ref), custom_call_target="tpu_custom_call" | custom-call | flops 8589934592 | bytes 16777216 | tf_op jit(solution)/shard_map/pallas_call | solution.py:378
  108.1 1.1 collective-permute-start.1
  109.3 3.9 %collective-permute-done.1 = bf16[64,8,256]{2,1,0:T(8,128)(2,1)S(1)} collective-permute-done((bf16[64,8,256]{2,1,0:T(8,128)(2,1)S(1)}, bf16[64,8,256]{2,1,0:T(8,128)(2,1)S(1)}, u32[]{:S(2)}, u32[]{:S(2)}) %collective-permute-start.1) | collective-permute-done | bytes 262176 | tf_op jit(solution)/shard_map/ppermute | solution.py:18
  113.1 0.8 fusion
  (8 shorter events, 0.1 us)
Async XLA Ops:
  6.5 1.6 %copy-start = (bf16[8,64,8,256]{3,2,1,0:T(8,128)(2,1)S(1)}, bf16[8,64,8,256]{3,2,1,0:T(8,128)(2,1)}, u32[]{:S(2)}) copy-start(bf16[8,64,8,256]{3,2,1,0:T(8,128)(2,1)} %param.11) | copy-start | bytes 6291460
  6.5 55.3 %all-gather.2.cloned.1.call-start = ((), (), s32[]{:S(2)}) async-start(), calls=%async_computation.1 | async-start | bytes 2359296 | tf_op jit(solution)/shard_map/all_gather | solution.py:163
  23.9 7.0 %collective-permute-start = (bf16[1,64,8,256]{3,2,1,0:T(8,128)(2,1)}, bf16[1,64,8,256]{3,2,1,0:T(8,128)(2,1)S(1)}, u32[]{:S(2)}, u32[]{:S(2)}) collective-permute-start(bf16[1,64,8,256]{3,2,1,0:T(8,128)(2,1)} %param.6), channel_id=1, source_target_pairs={{28,0},{0,4},{4,8},{8,12},{12,16},{16,20},{20,24},{24,28},{29,1},{... | collective-permute-start | bytes 786440 | tf_op jit(solution)/shard_map/ppermute | solution.py:18
  27.0 3.8 %copy-start.2 = (bf16[1,64,8,256]{3,2,1,0:T(8,128)(2,1)S(1)}, bf16[1,64,8,256]{3,2,1,0:T(8,128)(2,1)}, u32[]{:S(2)}) copy-start(bf16[1,64,8,256]{3,2,1,0:T(8,128)(2,1)} %param.6) | copy-start | bytes 786436
  60.9 1.0 copy-start.4
  61.8 2.3 %copy-start.1 = (bf16[1,2,256,8,256]{4,2,3,1,0:T(8,128)(2,1)S(1)}, bf16[1,2,256,8,256]{4,2,3,1,0:T(8,128)(2,1)}, u32[]{:S(2)}) copy-start(bf16[1,2,256,8,256]{4,2,3,1,0:T(8,128)(2,1)} %copy.38) | copy-start | bytes 6291460
  61.8 2.3 %copy-start.3 = (s32[1,256,128]{2,1,0:T(8,128)S(1)}, s32[1,256,128]{2,1,0:T(8,128)}, u32[]{:S(2)}) copy-start(s32[1,256,128]{2,1,0:T(8,128)} %param.9) | copy-start | bytes 393220
  61.8 2.5 %copy-start.5 = (bf16[2048,256]{1,0:T(8,128)(2,1)S(1)}, bf16[2048,256]{1,0:T(8,128)(2,1)}, u32[]{:S(2)}) copy-start(bf16[2048,256]{1,0:T(8,128)(2,1)} %copy-done.4) | copy-start | bytes 3145732
  108.1 5.0 %collective-permute-start.1 = (bf16[64,8,256]{2,1,0:T(8,128)(2,1)S(1)}, bf16[64,8,256]{2,1,0:T(8,128)(2,1)S(1)}, u32[]{:S(2)}, u32[]{:S(2)}) collective-permute-start(bf16[64,8,256]{2,1,0:T(8,128)(2,1)S(1)} %bitcast.39), channel_id=1, source_target_pairs={{4,0},{8,4},{12,8},{16,12},{20,16},{24,20},{28,24},{0,28},{5,1},{9... | collective-permute-start | bytes 786440 | tf_op jit(solution)/shard_map/ppermute | solution.py:18
Sparse Core Ops, SparseCore 0:
  24.0 27.1 all-gather.1

commit v3 on v2

--- a/solution.py
+++ b/solution.py
@@ -10,6 +10,7 @@
 BLOCK = 64
 LANES = 128
 ROWS = 128
+LAG = 2
 
 
 def shifted(block, axis, distance):
@@ -43,14 +44,28 @@
 
 
 def coil_kernel(
-    moved_ref, sens_ref, kspace_ref, mask_ref, row_ref, back_ref, column_ref, out_ref,
-    wide_ref, sums_ref, send_ref, recv_ref, send_sem, recv_sem,
+    moved_ref, sens_ref, kspace_ref, mask_ref, row_ref, back_ref, column_ref, index_ref, w_hbm,
+    out_ref, pulled_ref,
+    wide_ref, sums_ref, send_ref, recv_ref, w_ref, expand_ref, spread_ref, warp_ref,
+    send_sem, recv_sem, load_sem,
 ):
     f32, bf16 = jnp.float32, jnp.bfloat16
     me, count = lax.axis_index("coil"), lax.axis_size("coil")
     coils, depth = sens_ref.shape[0], sens_ref.shape[1]
     own = NY // count
+    load = pltpu.make_async_copy(w_hbm, w_ref, load_sem)
+    load.start()
     meet("coil")
+    er = lax.broadcasted_iota(jnp.int32, (LANES, 8 * BLOCK), 0)
+    el = lax.broadcasted_iota(jnp.int32, (LANES, 8 * BLOCK), 1)
+    for s in range(2):
+        for h in range(2):
+            expand_ref[s * 2 + h] = one_hot(er == s * BLOCK + el % BLOCK // 2 * 2 + h)
+    mr = lax.broadcasted_iota(jnp.int32, (8, 8 * BLOCK), 0)
+    ml = lax.broadcasted_iota(jnp.int32, (8, 8 * BLOCK), 1)
+    masks = [(ml // BLOCK == mr) & (ml % 2 == k) for k in range(2)]
+    low = lax.broadcasted_iota(jnp.int32, (ROWS, LANES), 1) < BLOCK
+    low8 = low[:8]
     for part in range(2):
         wide_ref[part] = moved_ref[:, part * LANES : (part + 1) * LANES].astype(f32)
 
@@ -69,14 +84,16 @@
             device_id_type=pl.DeviceIdType.MESH,
         )
 
-    def one_depth(z, carry):
+    def one_depth(z):
         image_re = wide_ref[0, pl.ds(z, NY, stride=depth), :]
         image_im = wide_ref[1, pl.ds(z, NY, stride=depth), :]
         mask = mask_ref[...].astype(f32)
         mask = jnp.concatenate([mask, mask], axis=1)
         total_re = total_im = 0.0
         for c in range(coils):
-            sens = sens_ref[c, z].astype(f32)
+            sens = jnp.concatenate(
+                [sens_ref[c, z, lax.rem(me - w + count, count)] for w in range(count)], axis=0
+            ).astype(f32)
             sens_re, sens_im = sens[:, :LANES], sens[:, LANES:]
             coil_image = jnp.concatenate(
                 [
@@ -106,9 +123,8 @@
         send_ref[z] = jnp.concatenate([total_re, total_im], axis=1).astype(bf16)
         for step in range(1, count):
             transfer(step, z).start()
-        return carry
-
-    def collect(z, carry):
+
+    def adjoint_depth(z):
         rows = pl.ds(pl.multiple_of(me * own, own), own)
         total = send_ref[z, rows, :].astype(f32)
         for step in range(1, count):
@@ -118,51 +134,140 @@
             sums_ref[part, pl.ds(z, own, stride=depth), :] = total[
                 :, part * LANES : (part + 1) * LANES
             ]
+        grad = total.astype(bf16)
+        for s in range(2):
+            for h in range(2):
+                for c in range(2):
+                    spread_ref[s * 4 + c * 2 + h] = multiply(
+                        grad[:, c * LANES : (c + 1) * LANES], expand_ref[s * 2 + h]
+                    )
+
+        def one_group(q):
+            start = pl.multiple_of(q * 8, 8)
+            tiles = []
+            for s in range(2):
+                values = [spread_ref[s * 4 + ch, pl.ds(start, 8), :] for ch in range(4)]
+                left = jnp.concatenate(
+                    [jnp.where(masks[k], values[ch], 0.0) for k in range(2) for ch in range(4)],
+                    axis=0,
+                ).astype(bf16)
+                weights = w_ref[pl.ds(start, 8), z, s].reshape(8 * BLOCK, LANES)
+                tiles.append(multiply(left, weights))
+            for k in range(2):
+                for c in range(2):
+                    at = k * 32 + c * 16
+                    plain = jnp.where(low8, tiles[0][at : at + 8], tiles[1][at + 8 : at + 16])
+                    moved = jnp.where(low8, tiles[1][at : at + 8], tiles[0][at + 8 : at + 16])
+                    place = pl.ds(start * depth + z, 8, stride=depth)
+                    warp_ref[k * 2 + c, place, :] = plain + turn(moved)
+
+        def two_groups(step, carry):
+            one_group(step * 2)
+            one_group(step * 2 + 1)
+            return carry
+
+        lax.fori_loop(0, own // 16, two_groups, 0)
+
+    def forward_step(z, carry):
+        one_depth(z)
+
+        @pl.when(z >= LAG)
+        def _():
+            @pl.when(z == LAG)
+            def _():
+                load.wait()
+
+            adjoint_depth(z - LAG)
+
+        return carry
+
+    def last_step(z, carry):
+        adjoint_depth(z)
+        return carry
+
+    def sent(z, carry):
         for step in range(1, count):
             transfer(step, z).wait_send()
         return carry
 
-    lax.fori_loop(0, depth, one_depth, 0)
-    lax.fori_loop(0, depth, collect, 0)
+    lax.fori_loop(0, depth, forward_step, 0)
+    lax.fori_loop(depth - LAG, depth, last_step, 0)
     out_ref[...] = jnp.concatenate([sums_ref[0], sums_ref[1]], axis=1)
-
-
-def coil_gradient(moved, sens, kspace, mask, row_matrix, column_tables):
+    numbers = lax.broadcasted_iota(jnp.int32, (2 * ROWS, ROWS), 0)
+    for band in range(own * depth // ROWS):
+        part = pl.ds(band * ROWS, ROWS)
+        index = index_ref[:, part]
+        select = jnp.concatenate(
+            [one_hot(index[s : s + 1, :] == numbers) for s in range(2)], axis=1
+        )
+        terms = jnp.concatenate(
+            strips_to_parts(warp_ref[2, part, :], warp_ref[3, part, :], low), axis=0
+        )
+        upper = terms.astype(bf16)
+        lower = (terms - upper.astype(f32)).astype(bf16)
+        summed = multiply(select, upper) + multiply(select, lower)
+        parts = strips_to_parts(summed[:ROWS], summed[ROWS:], low)
+        pulled_ref[part, :] = jnp.concatenate(
+            [parts[0] + warp_ref[0, part, :], parts[1] + warp_ref[1, part, :]], axis=1
+        ).astype(bf16)
+    lax.fori_loop(0, depth, sent, 0)
+
+
+def coil_gradient(
+    moved, sens, kspace, mask, row_matrix, column_tables, index_rows, weights
+):
     count = lax.axis_size("coil")
     coils, depth = sens.shape[:2]
     own = NY // count
     vmem = pl.BlockSpec(memory_space=pltpu.VMEM)
     return pl.pallas_call(
         coil_kernel,
-        in_specs=[vmem] * 7,
-        out_specs=vmem,
-        out_shape=jax.ShapeDtypeStruct((own * depth, 2 * LANES), jnp.float32),
+        in_specs=[vmem] * 8 + [pl.BlockSpec(memory_space=pl.ANY)],
+        out_specs=[vmem] * 2,
+        out_shape=[
+            jax.ShapeDtypeStruct((own * depth, 2 * LANES), jnp.float32),
+            jax.ShapeDtypeStruct((own * depth, 2 * LANES), jnp.bfloat16),
+        ],
         scratch_shapes=[
             pltpu.VMEM((2, NY * depth, LANES), jnp.float32),
             pltpu.VMEM((2, own * depth, LANES), jnp.float32),
             pltpu.VMEM((depth, NY, 2 * LANES), jnp.bfloat16),
             pltpu.VMEM((count - 1, depth, own, 2 * LANES), jnp.bfloat16),
+            pltpu.VMEM((own, depth, 2, BLOCK, LANES), jnp.bfloat16),
+            pltpu.VMEM((4, LANES, 8 * BLOCK), jnp.bfloat16),
+            pltpu.VMEM((8, own, 8 * BLOCK), jnp.float32),
+            pltpu.VMEM((4, own * depth, LANES), jnp.float32),
             pltpu.SemaphoreType.DMA((count - 1, depth)),
             pltpu.SemaphoreType.DMA((count - 1, depth)),
+            pltpu.SemaphoreType.DMA,
         ],
         compiler_params=pltpu.CompilerParams(
-            collective_id=1, has_side_effects=True, vmem_limit_bytes=40 * 1024 * 1024
+            collective_id=1, has_side_effects=True, vmem_limit_bytes=48 * 1024 * 1024
         ),
         cost_estimate=pl.CostEstimate(
             flops=coils * 2**31, bytes_accessed=coils * 2**22, transcendentals=0
         ),
-    )(moved, sens, kspace, mask, row_matrix, row_matrix.T, column_tables)
+    )(
+        moved, sens, kspace, mask, row_matrix, row_matrix.T, column_tables, index_rows,
+        weights.reshape(own, depth, 2, BLOCK, LANES),
+    )
 
 
 def own_coil_maps(sensitivity):
     coils, row_count, depth, width = sensitivity.shape
     bins, count = lax.axis_size("bin"), lax.axis_size("coil")
-    share = row_count // bins
-    mine = lax.dynamic_slice_in_dim(sensitivity, lax.axis_index("bin") * share, share, axis=1)
-    swapped = lax.all_to_all(mine, "coil", split_axis=0, concat_axis=1, tiled=True)
-    full = lax.all_gather(swapped, "bin", axis=0, tiled=False)
-    full = full.reshape(bins, coils // count, count, share, depth, width)
-    return full.transpose(1, 4, 2, 0, 3, 5).reshape(coils // count, depth, NY, width)
+    share, held = row_count // bins, coils // count
+    me = lax.axis_index("coil")
+    first = lax.axis_index("bin") * share
+    parts = []
+    for step in range(count):
+        target = lax.rem(me + step, count)
+        part = lax.dynamic_slice(
+            sensitivity, (target * held, first, 0, 0), (held, share, depth, width)
+        )
+        parts.append(shifted(part, "coil", step) if step else part)
+    full = lax.all_gather(jnp.stack(parts), "bin", axis=0, tiled=False)
+    return full.transpose(2, 4, 1, 0, 3, 5).reshape(held, depth, count, row_count, width)
 
 
 def one_hot(test):
@@ -313,88 +418,6 @@
     lax.fori_loop(0, rows // 32, four_rows, 0)
 
 
-def adjoint_kernel(w_ref, grad_ref, index_ref, out_ref, spread_ref, own_ref, other_ref):
-    f32, bf16 = jnp.float32, jnp.bfloat16
-    rows = ROWS
-    low = lax.broadcasted_iota(jnp.int32, (rows, LANES), 1) < BLOCK
-    grad = grad_ref[...].astype(bf16)
-    er = lax.broadcasted_iota(jnp.int32, (LANES, 8 * BLOCK), 0)
-    el = lax.broadcasted_iota(jnp.int32, (LANES, 8 * BLOCK), 1)
-    for s in range(2):
-        for h in range(2):
-            expand = one_hot(er == s * BLOCK + el % BLOCK // 2 * 2 + h)
-            for c in range(2):
-                spread_ref[s * 4 + c * 2 + h] = jnp.dot(
-                    grad[:, c * LANES : (c + 1) * LANES], expand, preferred_element_type=f32
-                )
-
-    mr = lax.broadcasted_iota(jnp.int32, (8, 8 * BLOCK), 0)
-    ml = lax.broadcasted_iota(jnp.int32, (8, 8 * BLOCK), 1)
-    masks = [(ml // BLOCK == mr) & (ml % 2 == k) for k in range(2)]
-    low8 = low[:8]
-
-    def one_row(y):
-        start = pl.multiple_of(y * 8, 8)
-        tiles = []
-        for s in range(2):
-            values = [spread_ref[s * 4 + ch, pl.ds(start, 8), :] for ch in range(4)]
-            left = jnp.concatenate(
-                [jnp.where(masks[k], values[ch], 0.0) for k in range(2) for ch in range(4)],
-                axis=0,
-            ).astype(bf16)
-            weights = w_ref[pl.ds(start, 8), s].reshape(8 * BLOCK, LANES)
-            tiles.append(jnp.dot(left, weights, preferred_element_type=f32))
-        for k, ref in enumerate((own_ref, other_ref)):
-            for c in range(2):
-                at = k * 32 + c * 16
-                plain = jnp.where(low8, tiles[0][at : at + 8], tiles[1][at + 8 : at + 16])
-                moved = jnp.where(low8, tiles[1][at : at + 8], tiles[0][at + 8 : at + 16])
-                ref[c, pl.ds(start, 8), :] = plain + turn(moved)
-
-    def two_rows(step, carry):
-        one_row(step * 2)
-        one_row(step * 2 + 1)
-        return carry
-
-    lax.fori_loop(0, rows // 16, two_rows, 0)
-    numbers = lax.broadcasted_iota(jnp.int32, (2 * rows, rows), 0)
-    index = index_ref[...]
-    select = jnp.concatenate(
-        [one_hot(index[s : s + 1, :] == numbers) for s in range(2)], axis=1
-    )
-    terms = jnp.concatenate(strips_to_parts(other_ref[0], other_ref[1], low), axis=0)
-    upper = terms.astype(bf16)
-    lower = (terms - upper.astype(f32)).astype(bf16)
-    summed = jnp.dot(select, upper, preferred_element_type=f32) + jnp.dot(
-        select, lower, preferred_element_type=f32
-    )
-    parts = strips_to_parts(summed[:rows], summed[rows:], low)
-    out_ref[...] = jnp.concatenate(
-        [parts[0] + own_ref[0], parts[1] + own_ref[1]], axis=1
-    ).astype(bf16)
-
-
-def band_call(kernel, bands, inputs, specs, scratch, flops, moved):
-    return pl.pallas_call(
-        kernel,
-        grid=(bands,),
-        in_specs=specs,
-        out_specs=pl.BlockSpec((ROWS, 2 * LANES), lambda b: (b, 0)),
-        out_shape=jax.ShapeDtypeStruct((bands * ROWS, 2 * LANES), jnp.bfloat16),
-        scratch_shapes=scratch,
-        compiler_params=pltpu.CompilerParams(vmem_limit_bytes=40 * 1024 * 1024),
-        cost_estimate=pl.CostEstimate(flops=flops, bytes_accessed=moved, transcendentals=0),
-    )(*inputs)
-
-
-def weight_spec():
-    return pl.BlockSpec((ROWS, 2, BLOCK, LANES), lambda b: (b, 0, 0, 0))
-
-
-def image_spec():
-    return pl.BlockSpec((ROWS, 2 * LANES), lambda b: (b, 0))
-
-
 def warp_forward(earlier, current, weights, index_columns):
     count = lax.axis_size("coil")
     rows = earlier.shape[0]
@@ -421,23 +444,6 @@
     )(weights, earlier, current, index_columns)
 
 
-def warp_adjoint(grad, weights, index_rows):
-    bands = grad.shape[0] // ROWS
-    return band_call(
-        adjoint_kernel,
-        bands,
-        (weights, grad, index_rows),
-        [weight_spec(), image_spec(), pl.BlockSpec((2, ROWS), lambda b: (0, b))],
-        [
-            pltpu.VMEM((8, ROWS, 8 * BLOCK), jnp.float32),
-            pltpu.VMEM((2, ROWS, LANES), jnp.float32),
-            pltpu.VMEM((2, ROWS, LANES), jnp.float32),
-        ],
-        bands * 2**31,
-        bands * 2**22,
-    )
-
-
 def arrange_weights(blocks):
     count = blocks.shape[0]
     lines = blocks.reshape(count, 2, BLOCK * BLOCK // LANES, LANES)
@@ -463,10 +469,10 @@
     moved_image = warp_forward(
         earlier.reshape(flat_shape), current.reshape(flat_shape), weights, places
     )
-    data_grad = coil_gradient(
-        moved_image, sens, kspace, sample_mask[0], row_matrix, column_tables
+    data_grad, pulled = coil_gradient(
+        moved_image, sens, kspace, sample_mask[0], row_matrix, column_tables, places.T, weights
     )
-    pulled = warp_adjoint(data_grad, weights, places.T).reshape(current.shape)
+    pulled = pulled.reshape(current.shape)
     from_next = shifted(pulled, "bin", -1)
     return (data_grad.reshape(current.shape) + from_next.astype(jnp.float32))[None]
 

time: 121 us -> 106 us (0.88); the launches traced: 121 us -> 105 us
  blocking collectives: 15 us -> 0 us
  Pallas kernels: 73.8 us -> 64.1 us
  waiting for transfers between devices: 4.26 us -> 9.57 us
  starting transfers between devices: 1.19 us -> 6.23 us
  local copies, waits for them, and re-layouts: 10.5 us -> 7.78 us
    all_to_all x1 -> x0, blocking collectives: 15 us -> none  [own_coil_maps(): lax.all_to_all(mine, 'coil', split_axis=0, concat_axis=1, tiled=True)]
    pallas_call x2 -> x1, Pallas kernels: 43.7 us -> 34.1 us  [coil_gradient(): pl.pallas_call(coil_kernel, in_specs=[vmem] * 8 + [pl.BlockSpec(memory_sp...]
    ppermute x2 -> x5, waiting for transfers between devices: 4.25 us -> 9.53 us  [shifted(): return lax.ppermute(block, axis, route)]
    ppermute x2 -> x5, starting transfers between devices: 1.19 us -> 6.23 us  [shifted(): return lax.ppermute(block, axis, route)]
    unnamed x13 -> x5, local copies, waits for them, and re-layouts: 6.24 us -> 3.42 us
    transpose x1 -> x0, local copies, waits for them, and re-layouts: 2.24 us -> none  [own_coil_maps(): full.transpose(1, 4, 2, 0, 3, 5).reshape(coils // count, depth, NY, width)]
    all_gather x0 -> x1, local copies, waits for them, and re-layouts: none -> 2.12 us  [own_coil_maps(): full = lax.all_gather(jnp.stack(parts), 'bin', axis=0, tiled=False)]
  transfers between devices with their start and end apart: 3 -> 6, of which waited for: 2 -> 5; matrix products, arithmetic and copies ran while one was open for 5% -> 6% of each run, Pallas kernels for 25% -> 29%
where the time goes in v3:
time: 106 us; the launch traced here: 105 us
  Pallas kernels  64.1 us (60%)
  between operations  13.5 us (13%)
  waiting for transfers between devices  9.57 us (9%)
  local copies, waits for them, and re-layouts  7.78 us (7%)
  starting transfers between devices  6.23 us (6%)
  other arithmetic  3.35 us (3%)
    pallas_call x1, Pallas kernels, coil_gradient(): pl.pallas_call(coil_kernel, in_specs=[vmem] * 8 + [pl.BlockSpec(memory_sp...  34.1 us
    pallas_call x1, Pallas kernels, warp_forward(): pl.pallas_call(forward_kernel, in_specs=[pl.BlockSpec(memory_space=pl.ANY...  30 us
    ppermute x5, waiting for transfers between devices, shifted(): return lax.ppermute(block, axis, route)  9.53 us
    ppermute x5, starting transfers between devices, shifted(): return lax.ppermute(block, axis, route)  6.23 us
    unnamed x5, local copies, waits for them, and re-layouts  3.42 us
    all_gather x1, local copies, waits for them, and re-layouts, own_coil_maps(): full = lax.all_gather(jnp.stack(parts), 'bin', axis=0, tiled=False)  2.12 us
  transfers between devices with their start and end apart: 6, of which 5 were waited for; matrix products, arithmetic and copies ran while one was open for 6% of the time, Pallas kernels for 29%

profile of v3, /device:TPU:0, one launch (start us, length us, event | category | flops | bytes accessed | tf_op | source)
XLA Modules:
  0.0 104.6 jit_solution(16732246558531546641)
XLA Ops:
  6.5 0.0 all-gather.3.cloned.1.call-start
  6.5 1.0 dynamic-slice_bitcast_fusion
  7.5 3.1 %collective-permute-start.1 = (bf16[2,8,8,256]{3,2,1,0:T(8,128)(2,1)S(1)}, bf16[2,8,8,256]{3,2,1,0:T(8,128)(2,1)S(1)}, u32[]{:S(2)}, u32[]{:S(2)}) collective-permute-start(bf16[2,8,8,256]{3,2,1,0:T(8,128)(2,1)S(1)} %get-tuple-element.10), channel_id=1, source_target_pairs={{3,0},{0,1},{1,2},{2,3},{7,4},{4,5},{5,6},{6,7},{11,8},{8,9},{9,10... | collective-permute-start | bytes 196616 | tf_op jit(solution)/shard_map/ppermute | solution.py:19
  10.6 2.1 %collective-permute-start.3 = (bf16[2,8,8,256]{3,2,1,0:T(8,128)(2,1)S(1)}, bf16[2,8,8,256]{3,2,1,0:T(8,128)(2,1)S(1)}, u32[]{:S(2)}, u32[]{:S(2)}) collective-permute-start(bf16[2,8,8,256]{3,2,1,0:T(8,128)(2,1)S(1)} %get-tuple-element.11), channel_id=1, source_target_pairs={{1,0},{2,1},{3,2},{0,3},{5,4},{6,5},{7,6},{4,7},{9,8},{10,9},{11,1... | collective-permute-start | bytes 196616 | tf_op jit(solution)/shard_map/ppermute | solution.py:19
  12.7 0.9 collective-permute-start.2
  13.6 1.4 %collective-permute-done.1 = bf16[2,8,8,256]{3,2,1,0:T(8,128)(2,1)S(1)} collective-permute-done((bf16[2,8,8,256]{3,2,1,0:T(8,128)(2,1)S(1)}, bf16[2,8,8,256]{3,2,1,0:T(8,128)(2,1)S(1)}, u32[]{:S(2)}, u32[]{:S(2)}) %collective-permute-start.1) | collective-permute-done | bytes 65568 | tf_op jit(solution)/shard_map/ppermute | solution.py:19
  15.0 0.5 collective-permute-done.3
  15.5 3.4 %collective-permute-done.2 = bf16[2,8,8,256]{3,2,1,0:T(8,128)(2,1)S(1)} collective-permute-done((bf16[2,8,8,256]{3,2,1,0:T(8,128)(2,1)S(1)}, bf16[2,8,8,256]{3,2,1,0:T(8,128)(2,1)S(1)}, u32[]{:S(2)}, u32[]{:S(2)}) %collective-permute-start.2) | collective-permute-done | bytes 65568 | tf_op jit(solution)/shard_map/ppermute | solution.py:19
  18.9 0.7 pad_maximum_fusion
  19.6 0.0 all-gather.3.cloned.1.call-update
  19.7 0.1 collective-permute-start
  19.7 0.7 slice_reduce_fusion
  20.4 0.2 squeeze.13
  20.7 0.1 copy.21
  20.8 0.3 fusion.13
  21.0 0.3 negate_convert_fusion
  21.3 1.1 %multiply_convert_fusion = (bf16[1,256,256]{2,1,0:T(8,128)(2,1)S(1)}, bf16[1,256,256]{2,1,0:T(8,128)(2,1)S(1)}) fusion(), kind=kLoop, calls=%fused_computation.12 | loop fusion | flops 1179648 | bytes 262144 | tf_op jit(solution)/shard_map/convert.1
  22.5 0.1 copy.27.row_ref
  22.7 0.2 copy.24.index_ref
  22.8 0.0 copy-start.1
  22.8 3.4 %copy.30 = bf16[1,2,256,8,256]{4,2,3,1,0:T(8,128)(2,1)} copy(bf16[1,2,256,8,256]{4,3,2,1,0:T(8,128)(2,1)} %param.10) | data formatting | bytes 4194304 | tf_op args[4]
  26.3 0.4 collective-permute-done
  26.6 0.0 copy-done.1
  26.6 30.0 %shard_map.64.moved_ref = bf16[2048,256]{1,0:T(8,128)(2,1)S(1)} custom-call(bf16[512,2,64,128]{3,2,1,0:T(8,128)(2,1)} %bitcast.45, bf16[512,256]{1,0:T(8,128)(2,1)S(1)} %bitcast.43, bf16[512,256]{1,0:T(8,128)(2,1)S(1)} %bitcast.42, s32[512,2]{1,0:T(8,128)S(1)} %copy.24.index_ref), custom_call_target="tpu_custom_call" | custom-call | flops 8589934592 | bytes 16777216 | tf_op jit(solution)/shard_map/pallas_call | solution.py:426
  56.6 0.0 all-gather.3.cloned.1.call-done
  56.7 0.0 copy-start
  56.7 2.1 %copy.31 = bf16[8,4,2,8,8,256]{5,3,0,1,4,2:T(8,128)(2,1)S(1)} copy(bf16[8,4,2,8,8,256]{5,4,3,2,1,0:T(8,128)(2,1)} %bitcast.48) | data formatting | bytes 4194304 | tf_op jit(solution)/shard_map/all_gather | solution.py:269
  58.8 0.0 copy-done
  58.8 34.1 %shard_map.65 = (f32[512,256]{1,0:T(8,128)S(1)}, bf16[512,256]{1,0:T(8,128)(2,1)S(1)}) custom-call(bf16[2048,256]{1,0:T(8,128)(2,1)S(1)} %shard_map.64.moved_ref, bf16[2,8,4,64,256]{4,3,2,1,0:T(8,128)(2,1)S(1)} %bitcast.39, bf16[2,8,256,256]{3,2,1,0:T(8,128)(2,1)} %bitcast.47, s32[256,128]{1,0:T(8,128)S(1)} %bitcast.41, bf16[256,256]{1,0:T(8,128)(2,1)S(1)} %copy.27.row_ref, ...), custom_call_target="tpu_custom_call" | custom-call | flops 4294967296 | bytes 8388608 | tf_op jit(solution)/shard_map/pallas_call | solution.py:223
  93.0 0.1 collective-permute-start.4
  93.0 3.9 %collective-permute-done.4 = bf16[64,8,256]{2,1,0:T(8,128)(2,1)S(1)} collective-permute-done((bf16[64,8,256]{2,1,0:T(8,128)(2,1)S(1)}, bf16[64,8,256]{2,1,0:T(8,128)(2,1)S(1)}, u32[]{:S(2)}, u32[]{:S(2)}) %collective-permute-start.4) | collective-permute-done | bytes 262176 | tf_op jit(solution)/shard_map/ppermute | solution.py:19
  96.9 0.8 fusion
  (4 shorter events, 0.1 us)
Async XLA Ops:
  6.5 50.1 %all-gather.3.cloned.1.call-start = ((), (), s32[]{:S(2)}) async-start(), calls=%async_computation | async-start | bytes 2359296 | tf_op jit(solution)/shard_map/all_gather | solution.py:269
  7.5 7.5 %collective-permute-start.1 = (bf16[2,8,8,256]{3,2,1,0:T(8,128)(2,1)S(1)}, bf16[2,8,8,256]{3,2,1,0:T(8,128)(2,1)S(1)}, u32[]{:S(2)}, u32[]{:S(2)}) collective-permute-start(bf16[2,8,8,256]{3,2,1,0:T(8,128)(2,1)S(1)} %get-tuple-element.10), channel_id=1, source_target_pairs={{3,0},{0,1},{1,2},{2,3},{7,4},{4,5},{5,6},{6,7},{11,8},{8,9},{9,10... | collective-permute-start | bytes 196616 | tf_op jit(solution)/shard_map/ppermute | solution.py:19
  10.6 5.0 %collective-permute-start.3 = (bf16[2,8,8,256]{3,2,1,0:T(8,128)(2,1)S(1)}, bf16[2,8,8,256]{3,2,1,0:T(8,128)(2,1)S(1)}, u32[]{:S(2)}, u32[]{:S(2)}) collective-permute-start(bf16[2,8,8,256]{3,2,1,0:T(8,128)(2,1)S(1)} %get-tuple-element.11), channel_id=1, source_target_pairs={{1,0},{2,1},{3,2},{0,3},{5,4},{6,5},{7,6},{4,7},{9,8},{10,9},{11,1... | collective-permute-start | bytes 196616 | tf_op jit(solution)/shard_map/ppermute | solution.py:19
  12.7 6.2 %collective-permute-start.2 = (bf16[2,8,8,256]{3,2,1,0:T(8,128)(2,1)S(1)}, bf16[2,8,8,256]{3,2,1,0:T(8,128)(2,1)S(1)}, u32[]{:S(2)}, u32[]{:S(2)}) collective-permute-start(bf16[2,8,8,256]{3,2,1,0:T(8,128)(2,1)S(1)} %get-tuple-element.12), channel_id=1, source_target_pairs={{2,0},{3,1},{0,2},{1,3},{6,4},{7,5},{4,6},{5,7},{10,8},{11,9},{8,1... | collective-permute-start | bytes 196616 | tf_op jit(solution)/shard_map/ppermute | solution.py:19
  19.7 7.0 %collective-permute-start = (bf16[1,64,8,256]{3,2,1,0:T(8,128)(2,1)}, bf16[1,64,8,256]{3,2,1,0:T(8,128)(2,1)S(1)}, u32[]{:S(2)}, u32[]{:S(2)}) collective-permute-start(bf16[1,64,8,256]{3,2,1,0:T(8,128)(2,1)} %param.6), channel_id=1, source_target_pairs={{28,0},{0,4},{4,8},{8,12},{12,16},{16,20},{20,24},{24,28},{29,1},{... | collective-permute-start | bytes 786440 | tf_op jit(solution)/shard_map/ppermute | solution.py:19
  22.8 3.8 %copy-start.1 = (bf16[1,64,8,256]{3,2,1,0:T(8,128)(2,1)S(1)}, bf16[1,64,8,256]{3,2,1,0:T(8,128)(2,1)}, u32[]{:S(2)}) copy-start(bf16[1,64,8,256]{3,2,1,0:T(8,128)(2,1)} %param.6) | copy-start | bytes 786436
  56.7 2.1 %copy-start = (s32[1,256,128]{2,1,0:T(8,128)S(1)}, s32[1,256,128]{2,1,0:T(8,128)}, u32[]{:S(2)}) copy-start(s32[1,256,128]{2,1,0:T(8,128)} %param.9) | copy-start | bytes 393220
  93.0 3.9 %collective-permute-start.4 = (bf16[64,8,256]{2,1,0:T(8,128)(2,1)S(1)}, bf16[64,8,256]{2,1,0:T(8,128)(2,1)S(1)}, u32[]{:S(2)}, u32[]{:S(2)}) collective-permute-start(bf16[64,8,256]{2,1,0:T(8,128)(2,1)S(1)} %bitcast.44), channel_id=1, source_target_pairs={{4,0},{8,4},{12,8},{16,12},{20,16},{24,20},{28,24},{0,28},{5,1},{9... | collective-permute-start | bytes 786440 | tf_op jit(solution)/shard_map/ppermute | solution.py:19
Sparse Core Ops, SparseCore 0:
  19.8 27.8 all-gather.2

commit v4 on v3

--- a/solution.py
+++ b/solution.py
@@ -55,7 +55,7 @@
     own = NY // count
     load = pltpu.make_async_copy(w_hbm, w_ref, load_sem)
     load.start()
-    meet("coil")
+    meet(peers_of("coil"))
     er = lax.broadcasted_iota(jnp.int32, (LANES, 8 * BLOCK), 0)
     el = lax.broadcasted_iota(jnp.int32, (LANES, 8 * BLOCK), 1)
     for s in range(2):
@@ -161,12 +161,14 @@
                     place = pl.ds(start * depth + z, 8, stride=depth)
                     warp_ref[k * 2 + c, place, :] = plain + turn(moved)
 
-        def two_groups(step, carry):
-            one_group(step * 2)
-            one_group(step * 2 + 1)
+        together = min(4, own // 8)
+
+        def some_groups(step, carry):
+            for i in range(together):
+                one_group(step * together + i)
             return carry
 
-        lax.fori_loop(0, own // 16, two_groups, 0)
+        lax.fori_loop(0, own // 8 // together, some_groups, 0)
 
     def forward_step(z, carry):
         one_depth(z)
@@ -253,21 +255,9 @@
     )
 
 
-def own_coil_maps(sensitivity):
-    coils, row_count, depth, width = sensitivity.shape
-    bins, count = lax.axis_size("bin"), lax.axis_size("coil")
-    share, held = row_count // bins, coils // count
-    me = lax.axis_index("coil")
-    first = lax.axis_index("bin") * share
-    parts = []
-    for step in range(count):
-        target = lax.rem(me + step, count)
-        part = lax.dynamic_slice(
-            sensitivity, (target * held, first, 0, 0), (held, share, depth, width)
-        )
-        parts.append(shifted(part, "coil", step) if step else part)
-    full = lax.all_gather(jnp.stack(parts), "bin", axis=0, tiled=False)
-    return full.transpose(2, 4, 1, 0, 3, 5).reshape(held, depth, count, row_count, width)
+def arrange_maps(maps):
+    bins, count, held, share, depth, width = maps.shape
+    return maps.transpose(2, 4, 1, 0, 3, 5).reshape(held, depth, count, bins * share, width)
 
 
 def one_hot(test):
@@ -282,22 +272,24 @@
     return jnp.where(low, first, turn(second)), jnp.where(low, turn(first), second)
 
 
-def meet(axis):
+def peers_of(axis):
     me, count = lax.axis_index(axis), lax.axis_size(axis)
+    return [{axis: lax.rem(me + step, count)} for step in range(1, count)]
+
+
+def meet(peers):
     barrier = pltpu.get_barrier_semaphore()
-    for step in range(1, count):
+    for peer in peers:
         pl.semaphore_signal(
-            barrier,
-            inc=1,
-            device_id={axis: lax.rem(me + step, count)},
-            device_id_type=pl.DeviceIdType.MESH,
-        )
-    pl.semaphore_wait(barrier, count - 1)
+            barrier, inc=1, device_id=peer, device_id_type=pl.DeviceIdType.MESH
+        )
+    pl.semaphore_wait(barrier, len(peers))
 
 
 def forward_kernel(
-    w_hbm, earlier_ref, current_ref, index_ref, out_ref, w_buffer, source_ref,
-    load_sem, send_sem, recv_sem,
+    w_hbm, sens_hbm, earlier_ref, current_ref, index_ref, out_ref, maps_ref,
+    w_buffer, source_ref, load_sem, send_sem, recv_sem,
+    own_sem, coil_send, coil_recv, bin_send, bin_recv,
 ):
     me, count = lax.axis_index("coil"), lax.axis_size("coil")
     total_rows = current_ref.shape[0]
@@ -309,8 +301,30 @@
             w_hbm.at[pl.ds(b * ROWS, ROWS)], w_buffer.at[b % 2], load_sem.at[b % 2]
         )
 
+    my_bin = lax.axis_index("bin")
+    held, share = maps_ref.shape[2:4]
+
+    def coil_part(target):
+        return sens_hbm.at[pl.ds(target * held, held), pl.ds(my_bin * share, share)]
+
     load(0).start()
-    meet("coil")
+    own_maps = pltpu.make_async_copy(coil_part(me), maps_ref.at[my_bin, 0], own_sem)
+    own_maps.start()
+    meet(peers_of("coil") + peers_of("bin"))
+    swaps = []
+    for step in range(1, count):
+        target = lax.rem(me + step, count)
+        swaps.append(
+            pltpu.make_async_remote_copy(
+                src_ref=coil_part(target),
+                dst_ref=maps_ref.at[my_bin, step],
+                send_sem=coil_send.at[step - 1],
+                recv_sem=coil_recv.at[step - 1],
+                device_id={"coil": target},
+                device_id_type=pl.DeviceIdType.MESH,
+            )
+        )
+        swaps[-1].start()
     sends = []
     for b in range(bands):
         load(b).wait()
@@ -337,6 +351,21 @@
             )
             copy.start()
             sends.append(copy)
+        if b == 0:
+            own_maps.wait()
+            for copy in swaps:
+                copy.wait()
+            for step, peer in enumerate(peers_of("bin")):
+                copy = pltpu.make_async_remote_copy(
+                    src_ref=maps_ref.at[my_bin],
+                    dst_ref=maps_ref.at[my_bin],
+                    send_sem=bin_send.at[step],
+                    recv_sem=bin_recv.at[step],
+                    device_id=peer,
+                    device_id_type=pl.DeviceIdType.MESH,
+                )
+                copy.start()
+                sends.append(copy)
     for copy in sends:
         copy.wait()
 
@@ -418,22 +447,32 @@
     lax.fori_loop(0, rows // 32, four_rows, 0)
 
 
-def warp_forward(earlier, current, weights, index_columns):
-    count = lax.axis_size("coil")
+def warp_forward(earlier, current, weights, index_columns, sensitivity):
+    count, bins = lax.axis_size("coil"), lax.axis_size("bin")
+    coils, row_count, depth, width = sensitivity.shape
+    held, share = coils // count, row_count // bins
     rows = earlier.shape[0]
     bands = rows // ROWS
     vmem = pl.BlockSpec(memory_space=pltpu.VMEM)
     return pl.pallas_call(
         forward_kernel,
-        in_specs=[pl.BlockSpec(memory_space=pl.ANY), vmem, vmem, vmem],
-        out_specs=vmem,
-        out_shape=jax.ShapeDtypeStruct((count * rows, 2 * LANES), jnp.bfloat16),
+        in_specs=[pl.BlockSpec(memory_space=pl.ANY)] * 2 + [vmem] * 3,
+        out_specs=[vmem] * 2,
+        out_shape=[
+            jax.ShapeDtypeStruct((count * rows, 2 * LANES), jnp.bfloat16),
+            jax.ShapeDtypeStruct((bins, count, held, share, depth, width), jnp.bfloat16),
+        ],
         scratch_shapes=[
             pltpu.VMEM((2, ROWS, 2, BLOCK, LANES), jnp.bfloat16),
             pltpu.VMEM((16, ROWS, 2 * LANES), jnp.float32),
             pltpu.SemaphoreType.DMA((2,)),
             pltpu.SemaphoreType.DMA((bands, count - 1)),
             pltpu.SemaphoreType.DMA((bands, count - 1)),
+            pltpu.SemaphoreType.DMA,
+            pltpu.SemaphoreType.DMA((count - 1,)),
+            pltpu.SemaphoreType.DMA((count - 1,)),
+            pltpu.SemaphoreType.DMA((bins - 1,)),
+            pltpu.SemaphoreType.DMA((bins - 1,)),
         ],
         compiler_params=pltpu.CompilerParams(
             collective_id=0, has_side_effects=True, vmem_limit_bytes=40 * 1024 * 1024
@@ -441,7 +480,7 @@
         cost_estimate=pl.CostEstimate(
             flops=bands * 2**31, bytes_accessed=bands * 2**22, transcendentals=0
         ),
-    )(weights, earlier, current, index_columns)
+    )(weights, sensitivity, earlier, current, index_columns)
 
 
 def arrange_weights(blocks):
@@ -461,14 +500,14 @@
     row_matrix = make_row_matrix(NX)
     column_tables = make_column_tables(NY).reshape(2 * NY, NY)
     earlier = shifted(cine_image, "bin", 1)[0]
-    sens = own_coil_maps(sensitivity)
     kspace = kspace_data[0].transpose(0, 2, 1, 3)
     weights = arrange_weights(warp_blocks[0])
     places = band_places(warp_index[0])
     flat_shape = (row_count * depth_count, full_width)
-    moved_image = warp_forward(
-        earlier.reshape(flat_shape), current.reshape(flat_shape), weights, places
+    moved_image, maps = warp_forward(
+        earlier.reshape(flat_shape), current.reshape(flat_shape), weights, places, sensitivity
     )
+    sens = arrange_maps(maps)
     data_grad, pulled = coil_gradient(
         moved_image, sens, kspace, sample_mask[0], row_matrix, column_tables, places.T, weights
     )

time: 106 us -> 81.9 us (0.77)
  between operations: 13.5 us -> 0.13 us
  local copies, waits for them, and re-layouts: 7.78 us -> 3.98 us
  starting transfers between devices: 6.23 us -> 2.52 us
  waiting for transfers between devices: 9.57 us -> 6.09 us
  Pallas kernels: 64.1 us -> 65.5 us
    ppermute x5 -> x2, starting transfers between devices: 6.23 us -> 2.52 us  [shifted(): return lax.ppermute(block, axis, route)]
    ppermute x5 -> x2, waiting for transfers between devices: 9.53 us -> 6.09 us  [shifted(): return lax.ppermute(block, axis, route)]
    pallas_call x1, Pallas kernels: 30 us -> 33.4 us  [warp_forward(): pl.pallas_call(forward_kernel, in_specs=[pl.BlockSpec(memory_space=pl.ANY...]
    all_gather x1 -> x0, local copies, waits for them, and re-layouts: 2.12 us -> none  [own_coil_maps(): full = lax.all_gather(jnp.stack(parts), 'bin', axis=0, tiled=False)]
    pallas_call x1, Pallas kernels: 34.1 us -> 32.1 us  [coil_gradient(): pl.pallas_call(coil_kernel, in_specs=[vmem] * 8 + [pl.BlockSpec(memory_sp...]
    unnamed x5 -> x9, local copies, waits for them, and re-layouts: 3.42 us -> 2.22 us
    another operation x4 -> x3, other arithmetic: 2.4 us -> 1.65 us
  transfers between devices with their start and end apart: 6 -> 2, of which waited for: 5 -> 2; matrix products, arithmetic and copies ran while one was open for 6% -> 6% of each run, Pallas kernels for 29% -> 0%
where the time goes in v4:
time: 81.9 us; the launch traced here: 80.9 us
  Pallas kernels  65.5 us (80%)
  waiting for transfers between devices  6.09 us (7%)
  local copies, waits for them, and re-layouts  3.98 us (5%)
  other arithmetic  2.62 us (3%)
  starting transfers between devices  2.52 us (3%)
    pallas_call x1, Pallas kernels, warp_forward(): pl.pallas_call(forward_kernel, in_specs=[pl.BlockSpec(memory_space=pl.ANY...  33.4 us
    pallas_call x1, Pallas kernels, coil_gradient(): pl.pallas_call(coil_kernel, in_specs=[vmem] * 8 + [pl.BlockSpec(memory_sp...  32.1 us
    ppermute x2, waiting for transfers between devices, shifted(): return lax.ppermute(block, axis, route)  6.09 us
    ppermute x2, starting transfers between devices, shifted(): return lax.ppermute(block, axis, route)  2.52 us
    unnamed x9, local copies, waits for them, and re-layouts  2.22 us
    another operation x3, other arithmetic  1.65 us
  transfers between devices with their start and end apart: 2, of which 2 were waited for; matrix products, arithmetic and copies ran while one was open for 6% of the time, Pallas kernels for 0%

profile of v4, /device:TPU:0, one launch (start us, length us, event | category | flops | bytes accessed | tf_op | source)
XLA Modules:
  0.0 80.9 jit_solution(1926534739079357653)
XLA Ops:
  0.0 0.0 copy-start.3
  0.0 0.5 collective-permute-start
  0.5 0.3 negate_convert_fusion
  0.7 0.3 fusion.13
  1.0 1.1 %multiply_convert_fusion = (bf16[1,256,256]{2,1,0:T(8,128)(2,1)S(1)}, bf16[1,256,256]{2,1,0:T(8,128)(2,1)S(1)}) fusion(), kind=kLoop, calls=%fused_computation.11 | loop fusion | flops 1179648 | bytes 262144 | tf_op jit(solution)/shard_map/convert.1
  2.1 0.7 slice_reduce_fusion
  2.8 0.2 squeeze.13
  3.0 0.1 copy.13
  3.3 0.1 copy.19.row_ref
  3.4 0.1 copy.16.index_ref
  3.5 0.0 copy-done.3
  3.5 0.0 copy-start.1
  3.5 0.0 copy-start.2
  3.6 1.8 %copy.22 = bf16[1,2,256,8,256]{4,2,3,1,0:T(8,128)(2,1)} copy(bf16[1,2,256,8,256]{4,3,2,1,0:T(8,128)(2,1)S(1)} %copy-done.3) | data formatting | bytes 4194304 | tf_op args[4]
  5.4 2.2 %collective-permute-done = bf16[1,64,8,256]{3,2,1,0:T(8,128)(2,1)S(1)} collective-permute-done((bf16[1,64,8,256]{3,2,1,0:T(8,128)(2,1)}, bf16[1,64,8,256]{3,2,1,0:T(8,128)(2,1)S(1)}, u32[]{:S(2)}, u32[]{:S(2)}) %collective-permute-start) | collective-permute-done | bytes 262176 | tf_op jit(solution)/shard_map/ppermute | solution.py:19
  7.6 0.0 copy-done.1
  7.6 0.0 copy-done.2
  7.6 33.4 %shard_map.64 = (bf16[2048,256]{1,0:T(8,128)(2,1)S(1)}, bf16[8,4,2,8,8,256]{5,4,3,2,1,0:T(8,128)(2,1)S(1)}) custom-call(bf16[512,2,64,128]{3,2,1,0:T(8,128)(2,1)} %bitcast.39, bf16[8,64,8,256]{3,2,1,0:T(8,128)(2,1)S(1)} %copy-done.1, bf16[512,256]{1,0:T(8,128)(2,1)S(1)} %bitcast.37, bf16[512,256]{1,0:T(8,128)(2,1)S(1)} %bitcast.36, s32[512,2]{1,0:T(8,128)S(1)} %copy.16.index_ref), custom_call_target="tpu_custom_call" | custom-call | flops 8589934592 | bytes 16777216 | tf_op jit(solution)/shard_map/pallas_call | solution.py:457
  41.1 0.0 copy-start
  41.1 0.5 copy.23
  41.6 0.4 copy-done
  42.0 32.1 %shard_map.65 = (f32[512,256]{1,0:T(8,128)S(1)}, bf16[512,256]{1,0:T(8,128)(2,1)S(1)}) custom-call(bf16[2048,256]{1,0:T(8,128)(2,1)S(1)} %get-tuple-element.9.moved_ref, bf16[2,8,4,64,256]{4,3,2,1,0:T(8,128)(2,1)S(1)} %bitcast.32, bf16[2,8,256,256]{3,2,1,0:T(8,128)(2,1)} %bitcast.41, s32[256,128]{1,0:T(8,128)S(1)} %bitcast.35, ...), custom_call_target="tpu_custom_call" | custom-call | flops 4294967296 | bytes 8388608 | tf_op jit(solution)/shard_map/pallas_call | solution.py:225
  74.1 2.1 %collective-permute-start.1 = (bf16[64,8,256]{2,1,0:T(8,128)(2,1)S(1)}, bf16[64,8,256]{2,1,0:T(8,128)(2,1)S(1)}, u32[]{:S(2)}, u32[]{:S(2)}) collective-permute-start(bf16[64,8,256]{2,1,0:T(8,128)(2,1)S(1)} %bitcast.38), channel_id=1, source_target_pairs={{4,0},{8,4},{12,8},{16,12},{20,16},{24,20},{28,24},{0,28},{5,1},{9... | collective-permute-start | bytes 786440 | tf_op jit(solution)/shard_map/ppermute | solution.py:19
  76.1 3.9 %collective-permute-done.1 = bf16[64,8,256]{2,1,0:T(8,128)(2,1)S(1)} collective-permute-done((bf16[64,8,256]{2,1,0:T(8,128)(2,1)S(1)}, bf16[64,8,256]{2,1,0:T(8,128)(2,1)S(1)}, u32[]{:S(2)}, u32[]{:S(2)}) %collective-permute-start.1) | collective-permute-done | bytes 262176 | tf_op jit(solution)/shard_map/ppermute | solution.py:19
  80.0 0.8 %fusion = f32[1,64,8,256]{3,2,1,0:T(8,128)} fusion(f32[512,256]{1,0:T(8,128)S(1)} %get-tuple-element.11, bf16[64,8,256]{2,1,0:T(8,128)(2,1)S(1)} %collective-permute-done.1), kind=kLoop, calls=%fused_computation.3 | loop fusion | flops 262144 | bytes 1310720 | tf_op jit(solution)/shard_map/broadcast_in_dim | solution.py:516
  (4 shorter events, 0.1 us)
Async XLA Ops:
  0.0 3.5 %copy-start.3 = (bf16[1,2,256,8,256]{4,3,2,1,0:T(8,128)(2,1)S(1)}, bf16[1,2,256,8,256]{4,3,2,1,0:T(8,128)(2,1)}, u32[]{:S(2)}) copy-start(bf16[1,2,256,8,256]{4,3,2,1,0:T(8,128)(2,1)} %param.10) | copy-start | bytes 6291460
  0.0 7.6 %collective-permute-start = (bf16[1,64,8,256]{3,2,1,0:T(8,128)(2,1)}, bf16[1,64,8,256]{3,2,1,0:T(8,128)(2,1)S(1)}, u32[]{:S(2)}, u32[]{:S(2)}) collective-permute-start(bf16[1,64,8,256]{3,2,1,0:T(8,128)(2,1)} %param.6), channel_id=1, source_target_pairs={{28,0},{0,4},{4,8},{8,12},{12,16},{16,20},{20,24},{24,28},{29,1},{... | collective-permute-start | bytes 786440 | tf_op jit(solution)/shard_map/ppermute | solution.py:19
  3.5 4.1 %copy-start.1 = (bf16[8,64,8,256]{3,2,1,0:T(8,128)(2,1)S(1)}, bf16[8,64,8,256]{3,2,1,0:T(8,128)(2,1)}, u32[]{:S(2)}) copy-start(bf16[8,64,8,256]{3,2,1,0:T(8,128)(2,1)} %sens_hbm.1) | copy-start | bytes 6291460
  3.5 4.1 %copy-start.2 = (bf16[1,64,8,256]{3,2,1,0:T(8,128)(2,1)S(1)}, bf16[1,64,8,256]{3,2,1,0:T(8,128)(2,1)}, u32[]{:S(2)}) copy-start(bf16[1,64,8,256]{3,2,1,0:T(8,128)(2,1)} %param.6) | copy-start | bytes 786436
  41.1 0.9 %copy-start = (s32[1,256,128]{2,1,0:T(8,128)S(1)}, s32[1,256,128]{2,1,0:T(8,128)}, u32[]{:S(2)}) copy-start(s32[1,256,128]{2,1,0:T(8,128)} %param.9) | copy-start | bytes 393220
  74.1 6.0 %collective-permute-start.1 = (bf16[64,8,256]{2,1,0:T(8,128)(2,1)S(1)}, bf16[64,8,256]{2,1,0:T(8,128)(2,1)S(1)}, u32[]{:S(2)}, u32[]{:S(2)}) collective-permute-start(bf16[64,8,256]{2,1,0:T(8,128)(2,1)S(1)} %bitcast.38), channel_id=1, source_target_pairs={{4,0},{8,4},{12,8},{16,12},{20,16},{24,20},{28,24},{0,28},{5,1},{9... | collective-permute-start | bytes 786440 | tf_op jit(solution)/shard_map/ppermute | solution.py:19

commit v5 on v4

--- a/solution.py
+++ b/solution.py
@@ -134,25 +134,24 @@
             sums_ref[part, pl.ds(z, own, stride=depth), :] = total[
                 :, part * LANES : (part + 1) * LANES
             ]
-        grad = total.astype(bf16)
+        grad = jnp.concatenate([total[:, :LANES], total[:, LANES:]], axis=0).astype(bf16)
         for s in range(2):
             for h in range(2):
+                spread = multiply(grad, expand_ref[s * 2 + h])
                 for c in range(2):
-                    spread_ref[s * 4 + c * 2 + h] = multiply(
-                        grad[:, c * LANES : (c + 1) * LANES], expand_ref[s * 2 + h]
-                    )
+                    spread_ref[s * 4 + c * 2 + h] = spread[c * own : (c + 1) * own]
 
         def one_group(q):
             start = pl.multiple_of(q * 8, 8)
-            tiles = []
+            left = []
             for s in range(2):
                 values = [spread_ref[s * 4 + ch, pl.ds(start, 8), :] for ch in range(4)]
-                left = jnp.concatenate(
-                    [jnp.where(masks[k], values[ch], 0.0) for k in range(2) for ch in range(4)],
-                    axis=0,
-                ).astype(bf16)
-                weights = w_ref[pl.ds(start, 8), z, s].reshape(8 * BLOCK, LANES)
-                tiles.append(multiply(left, weights))
+                left += [jnp.where(masks[k], values[ch], 0.0) for k in range(2) for ch in range(4)]
+            weights = jnp.concatenate(
+                [w_ref[pl.ds(start, 8), z, s].reshape(8 * BLOCK, LANES) for s in range(2)], axis=1
+            )
+            products = multiply(jnp.concatenate(left, axis=0).astype(bf16), weights)
+            tiles = [products[:BLOCK, :LANES], products[BLOCK:, LANES:]]
             for k in range(2):
                 for c in range(2):
                     at = k * 32 + c * 16
@@ -444,7 +443,7 @@
         two_rows(step * 2 + 1)
         return carry
 
-    lax.fori_loop(0, rows // 32, four_rows, 0)
+    lax.fori_loop(0, rows // 32, four_rows, 0, unroll=2)
 
 
 def warp_forward(earlier, current, weights, index_columns, sensitivity):

time: 81.9 us -> 81.9 us (level)
  no operation moved by 1% of the time
where the time goes in v5:
time: 81.9 us; the launch traced here: 81.2 us
  Pallas kernels  65.4 us (80%)
  waiting for transfers between devices  6.09 us (7%)
  local copies, waits for them, and re-layouts  3.98 us (5%)
  starting transfers between devices  3.04 us (4%)
  other arithmetic  2.62 us (3%)
    pallas_call x1, Pallas kernels, warp_forward(): pl.pallas_call(forward_kernel, in_specs=[pl.BlockSpec(memory_space=pl.ANY...  33.8 us
    pallas_call x1, Pallas kernels, coil_gradient(): pl.pallas_call(coil_kernel, in_specs=[vmem] * 8 + [pl.BlockSpec(memory_sp...  31.6 us
    ppermute x2, waiting for transfers between devices, shifted(): return lax.ppermute(block, axis, route)  6.09 us
    ppermute x2, starting transfers between devices, shifted(): return lax.ppermute(block, axis, route)  3.04 us
    unnamed x9, local copies, waits for them, and re-layouts  2.22 us
    another operation x3, other arithmetic  1.65 us
  transfers between devices with their start and end apart: 2, of which 2 were waited for; matrix products, arithmetic and copies ran while one was open for 6% of the time, Pallas kernels for 0%

profile of v5, /device:TPU:0, one launch (start us, length us, event | category | flops | bytes accessed | tf_op | source)
XLA Modules:
  0.0 81.2 jit_solution(8311847454635160460)
XLA Ops:
  0.0 0.0 copy-start.3
  0.0 0.5 collective-permute-start
  0.5 0.3 negate_convert_fusion
  0.7 0.3 fusion.13
  1.0 1.1 %multiply_convert_fusion = (bf16[1,256,256]{2,1,0:T(8,128)(2,1)S(1)}, bf16[1,256,256]{2,1,0:T(8,128)(2,1)S(1)}) fusion(), kind=kLoop, calls=%fused_computation.11 | loop fusion | flops 1179648 | bytes 262144 | tf_op jit(solution)/shard_map/convert.1
  2.1 0.7 slice_reduce_fusion
  2.8 0.2 squeeze.13
  3.0 0.1 copy.13
  3.3 0.1 copy.19.row_ref
  3.4 0.1 copy.16.index_ref
  3.5 0.0 copy-done.3
  3.5 0.0 copy-start.1
  3.5 0.0 copy-start.2
  3.6 1.8 %copy.22 = bf16[1,2,256,8,256]{4,2,3,1,0:T(8,128)(2,1)} copy(bf16[1,2,256,8,256]{4,3,2,1,0:T(8,128)(2,1)S(1)} %copy-done.3) | data formatting | bytes 4194304 | tf_op args[4]
  5.4 2.2 %collective-permute-done = bf16[1,64,8,256]{3,2,1,0:T(8,128)(2,1)S(1)} collective-permute-done((bf16[1,64,8,256]{3,2,1,0:T(8,128)(2,1)}, bf16[1,64,8,256]{3,2,1,0:T(8,128)(2,1)S(1)}, u32[]{:S(2)}, u32[]{:S(2)}) %collective-permute-start) | collective-permute-done | bytes 262176 | tf_op jit(solution)/shard_map/ppermute | solution.py:19
  7.6 0.0 copy-done.1
  7.6 0.0 copy-done.2
  7.6 33.8 %shard_map.64 = (bf16[2048,256]{1,0:T(8,128)(2,1)S(1)}, bf16[8,4,2,8,8,256]{5,4,3,2,1,0:T(8,128)(2,1)S(1)}) custom-call(bf16[512,2,64,128]{3,2,1,0:T(8,128)(2,1)} %bitcast.39, bf16[8,64,8,256]{3,2,1,0:T(8,128)(2,1)S(1)} %copy-done.1, bf16[512,256]{1,0:T(8,128)(2,1)S(1)} %bitcast.37, bf16[512,256]{1,0:T(8,128)(2,1)S(1)} %bitcast.36, s32[512,2]{1,0:T(8,128)S(1)} %copy.16.index_ref), custom_call_target="tpu_custom_call" | custom-call | flops 8589934592 | bytes 16777216 | tf_op jit(solution)/shard_map/pallas_call | solution.py:456
  41.4 0.0 copy-start
  41.4 0.5 copy.23
  41.9 0.4 copy-done
  42.3 31.6 %shard_map.65 = (f32[512,256]{1,0:T(8,128)S(1)}, bf16[512,256]{1,0:T(8,128)(2,1)S(1)}) custom-call(bf16[2048,256]{1,0:T(8,128)(2,1)S(1)} %get-tuple-element.9.moved_ref, bf16[2,8,4,64,256]{4,3,2,1,0:T(8,128)(2,1)S(1)} %bitcast.32, bf16[2,8,256,256]{3,2,1,0:T(8,128)(2,1)} %bitcast.41, s32[256,128]{1,0:T(8,128)S(1)} %bitcast.35, ...), custom_call_target="tpu_custom_call" | custom-call | flops 4294967296 | bytes 8388608 | tf_op jit(solution)/shard_map/pallas_call | solution.py:224
  73.9 2.6 %collective-permute-start.1 = (bf16[64,8,256]{2,1,0:T(8,128)(2,1)S(1)}, bf16[64,8,256]{2,1,0:T(8,128)(2,1)S(1)}, u32[]{:S(2)}, u32[]{:S(2)}) collective-permute-start(bf16[64,8,256]{2,1,0:T(8,128)(2,1)S(1)} %bitcast.38), channel_id=1, source_target_pairs={{4,0},{8,4},{12,8},{16,12},{20,16},{24,20},{28,24},{0,28},{5,1},{9... | collective-permute-start | bytes 786440 | tf_op jit(solution)/shard_map/ppermute | solution.py:19
  76.5 3.9 %collective-permute-done.1 = bf16[64,8,256]{2,1,0:T(8,128)(2,1)S(1)} collective-permute-done((bf16[64,8,256]{2,1,0:T(8,128)(2,1)S(1)}, bf16[64,8,256]{2,1,0:T(8,128)(2,1)S(1)}, u32[]{:S(2)}, u32[]{:S(2)}) %collective-permute-start.1) | collective-permute-done | bytes 262176 | tf_op jit(solution)/shard_map/ppermute | solution.py:19
  80.4 0.8 %fusion = f32[1,64,8,256]{3,2,1,0:T(8,128)} fusion(f32[512,256]{1,0:T(8,128)S(1)} %get-tuple-element.11, bf16[64,8,256]{2,1,0:T(8,128)(2,1)S(1)} %collective-permute-done.1), kind=kLoop, calls=%fused_computation.3 | loop fusion | flops 262144 | bytes 1310720 | tf_op jit(solution)/shard_map/broadcast_in_dim | solution.py:515
  (4 shorter events, 0.1 us)
Async XLA Ops:
  0.0 3.5 %copy-start.3 = (bf16[1,2,256,8,256]{4,3,2,1,0:T(8,128)(2,1)S(1)}, bf16[1,2,256,8,256]{4,3,2,1,0:T(8,128)(2,1)}, u32[]{:S(2)}) copy-start(bf16[1,2,256,8,256]{4,3,2,1,0:T(8,128)(2,1)} %param.10) | copy-start | bytes 6291460
  0.0 7.6 %collective-permute-start = (bf16[1,64,8,256]{3,2,1,0:T(8,128)(2,1)}, bf16[1,64,8,256]{3,2,1,0:T(8,128)(2,1)S(1)}, u32[]{:S(2)}, u32[]{:S(2)}) collective-permute-start(bf16[1,64,8,256]{3,2,1,0:T(8,128)(2,1)} %param.6), channel_id=1, source_target_pairs={{28,0},{0,4},{4,8},{8,12},{12,16},{16,20},{20,24},{24,28},{29,1},{... | collective-permute-start | bytes 786440 | tf_op jit(solution)/shard_map/ppermute | solution.py:19
  3.5 4.1 %copy-start.1 = (bf16[8,64,8,256]{3,2,1,0:T(8,128)(2,1)S(1)}, bf16[8,64,8,256]{3,2,1,0:T(8,128)(2,1)}, u32[]{:S(2)}) copy-start(bf16[8,64,8,256]{3,2,1,0:T(8,128)(2,1)} %sens_hbm.1) | copy-start | bytes 6291460
  3.5 4.1 %copy-start.2 = (bf16[1,64,8,256]{3,2,1,0:T(8,128)(2,1)S(1)}, bf16[1,64,8,256]{3,2,1,0:T(8,128)(2,1)}, u32[]{:S(2)}) copy-start(bf16[1,64,8,256]{3,2,1,0:T(8,128)(2,1)} %param.6) | copy-start | bytes 786436
  41.4 0.9 %copy-start = (s32[1,256,128]{2,1,0:T(8,128)S(1)}, s32[1,256,128]{2,1,0:T(8,128)}, u32[]{:S(2)}) copy-start(s32[1,256,128]{2,1,0:T(8,128)} %param.9) | copy-start | bytes 393220
  73.9 6.5 %collective-permute-start.1 = (bf16[64,8,256]{2,1,0:T(8,128)(2,1)S(1)}, bf16[64,8,256]{2,1,0:T(8,128)(2,1)S(1)}, u32[]{:S(2)}, u32[]{:S(2)}) collective-permute-start(bf16[64,8,256]{2,1,0:T(8,128)(2,1)S(1)} %bitcast.38), channel_id=1, source_target_pairs={{4,0},{8,4},{12,8},{16,12},{20,16},{24,20},{28,24},{0,28},{5,1},{9... | collective-permute-start | bytes 786440 | tf_op jit(solution)/shard_map/ppermute | solution.py:19
